TPU v7x, 32 devices: a whole 2x2x4 slice. The times are simulated.
32 devices in a mesh: outer: 2 (over x), role: 16 (over z, y, core).
Axes of the slice: x: 2, y: 2, z: 4, core: 2. Of those that a mesh axis runs over, the one named last changes fastest.
Arguments:
- images: bfloat16 [512, 5120], P(('outer', 'role')), parts along dimension 0, may hold values from -6 to 6
- vis_gain: float32 [5120], replicated, may hold values from 0.25 to 1.75
- w_merge: bfloat16 [5120, 8192], P(None, 'role'), may hold values from -0.078125 to 0.078125
- prompt_text: bfloat16 [7680, 8192], P(('outer', 'role')), parts along dimension 0, may hold values from -6 to 6
- norm_gain: float32 [8192], replicated, may hold values from 0.25 to 1.75
- w_kv: bfloat16 [8192, 2048], P('role'), may hold values from -0.0625 to 0.0625
- new_query: bfloat16 [32, 8192], P(('outer', 'role')), parts along dimension 0
- new_kv: bfloat16 [32, 2048], P(('outer', 'role')), parts along dimension 0
- text_len: int32 [32], P(('outer', 'role')), parts along dimension 0, may hold values from 1 to 240
- img_count: int32 [64], P(('outer', 'role')), parts along dimension 0, may hold values from 1 to 8
- img_dest: int32 [64, 1], P(('outer', 'role')), parts along dimension 0, may hold values from 0 to 15; in each aligned block of 32 rows (0 to 31, 32 to 63, ...) at most 4 rows name the same one
- block_dest: int32 [544, 1], P(('outer', 'role')), parts along dimension 0, may hold values from 0 to 15; in each aligned block of 17 rows (0 to 16, 17 to 33, ...) at most 2 rows name the same one
- past_cache: bfloat16 [1024, 16, 2048], P(('outer', 'role')), parts along dimension 0, may hold values from -6 to 6
- past_scale: bfloat16 [1024, 16], P(('outer', 'role')), parts along dimension 0, may hold values from 0.5 to 2
- past_owner: int32 [1024, 1], P(('outer', 'role')), parts along dimension 0, may hold values from 0 to 15; in each aligned block of 32 rows (0 to 31, 32 to 63, ...) at most 4 rows name the same one
Outputs:
- kv_cache: bfloat16 [1024, 16, 2048], P(('outer', 'role')), parts along dimension 0
- cache_scale: bfloat16 [1024, 16], P(('outer', 'role')), parts along dimension 0
- attended: bfloat16 [32, 8192], P(('outer', 'role')), parts along dimension 0
There are 2 independent parts, one for each index of `outer`. A program takes and returns all parts, laid end to end along the dimension named above; an argument that names none is the same for every part. Nothing has to cross between parts.
Inputs may be any that keep to these rules, and one draw needn't show every extreme that they name: `img_dest`: every prompt has one image or more and no prompt has more than 4; some prompt has exactly 4. `block_dest`: of one prompt's 17 blocks no rank takes more than 2; some rank takes exactly 2. `past_owner`: every request owns one earlier page or more.
All inputs are finite; a program needn't handle non-finite values.
Results may differ from a plain program's by a relative error of at most 0.0085.
Values may be sent and summed in bfloat16 or wider, within the bound.
A program may use at most 128 MiB of HBM per device.

v0:
```python
import math

import jax
import jax.numpy as jnp
from jax import lax
from jax.sharding import PartitionSpec as P

H = 64
KVH = 8
HD = 128
IMG_TOK = 8
IMGCAP = 4
BLK = 16


def joined(part, axis, combine):
    gathered = jax.tree.map(lambda a: lax.all_gather(a, axis), part)

    def take(source):
        return jax.tree.map(lambda a: lax.dynamic_index_in_dim(a, source, 0, False), gathered)

    return lax.fori_loop(
        1, lax.axis_size(axis), lambda source, state: combine(state, take(source)), take(0)
    )


def normalize(values, gain_vec):
    values = values.astype(jnp.float32)
    return values * lax.rsqrt(jnp.mean(values * values, axis=-1, keepdims=True) + 1e-06) * gain_vec


def rotate(key_part):
    halfway = HD // 2
    position = jnp.arange(key_part.shape[0]).astype(jnp.float32)
    inverse = jnp.exp(jnp.arange(halfway).astype(jnp.float32) * (-2.0 * math.log(1000000.0) / HD))
    angles = position[:, None] * inverse[None, :]
    cosine = jnp.cos(angles)[:, None, :]
    sine_part = jnp.sin(angles)[:, None, :]
    front_half = key_part[..., :halfway]
    back_half = key_part[..., halfway:]
    return jnp.concatenate(
        [front_half * cosine - back_half * sine_part, back_half * cosine + front_half * sine_part],
        axis=-1,
    )


def quantize(projected):
    length = projected.shape[0]
    key_part = rotate(projected[:, : KVH * HD].reshape(length, KVH, HD))
    value_part = projected[:, KVH * HD :].reshape(length, KVH, HD)
    stacked = jnp.stack([key_part, value_part], axis=1).reshape(length // BLK, BLK, 2, KVH, HD)
    largest = jnp.max(jnp.abs(stacked), axis=(1, 4))
    scales = ((largest + 1e-05) / 448.0).astype(jnp.bfloat16)
    quantized = (stacked / scales.astype(jnp.float32)[:, None, :, :, None]).astype(jnp.bfloat16)
    return (
        quantized.reshape(length // BLK, BLK, 2 * KVH * HD),
        scales.reshape(length // BLK, 2 * KVH),
    )


def combine(earlier, later):
    left_top, left_total, left_summed = earlier
    right_top, right_total, right_summed = later
    highest = jnp.maximum(left_top, right_top)
    left_factor = jnp.exp(left_top - highest)
    right_factor = jnp.exp(right_top - highest)
    return (
        highest,
        left_total * left_factor + right_total * right_factor,
        left_summed * left_factor[..., None] + right_summed * right_factor[..., None],
    )


def body(
    images,
    vis_gain,
    w_merge,
    prompt_text,
    norm_gain,
    w_kv,
    new_query,
    new_kv,
    text_len,
    img_count,
    img_dest,
    block_dest,
    past_cache,
    past_scale,
    past_owner,
):
    rank_count = lax.axis_size("role")
    myself = lax.axis_index("role")
    columns = w_merge.shape[1]
    groups = H // KVH
    factor = 1.0 / math.sqrt(HD)
    highest_prec = lax.Precision.HIGHEST
    normed_img = normalize(lax.all_gather(images, "role", axis=0, tiled=True), vis_gain).astype(
        jnp.bfloat16
    )
    merged = jnp.dot(normed_img, w_merge, preferred_element_type=jnp.float32).astype(jnp.bfloat16)
    counts, targets = (
        lax.all_gather(img_count, "role", axis=0, tiled=True),
        lax.all_gather(img_dest[:, 0], "role", axis=0, tiled=True),
    )
    image_total = targets.shape[0]
    chosen = (targets[:, None] == jnp.arange(rank_count)[None, :]).astype(jnp.int32)
    before = jnp.sum((jnp.cumsum(chosen, axis=0) - chosen) * chosen, axis=1)
    slot_of = targets * IMGCAP + before
    placing = (slot_of[None, :] == jnp.arange(rank_count * IMGCAP)[:, None]).astype(jnp.bfloat16)
    outgoing = jnp.dot(
        placing, merged.reshape(image_total, IMG_TOK * columns), preferred_element_type=jnp.float32
    )
    outgoing = outgoing.astype(jnp.bfloat16).reshape(rank_count, IMGCAP * IMG_TOK, columns)
    arrived = lax.all_to_all(outgoing, "role", split_axis=0, concat_axis=2, tiled=True)
    image_part = arrived.reshape(IMGCAP * IMG_TOK, rank_count * columns)
    is_mine = slot_of[None, :] == myself * IMGCAP + jnp.arange(IMGCAP)[:, None]
    slot_count = jnp.sum(jnp.where(is_mine, counts[None, :], 0), axis=1)
    image_valid = (jnp.arange(IMG_TOK)[None, :] < slot_count[:, None]).reshape(-1)
    text_valid = jnp.arange(prompt_text.shape[0]) < text_len[0]
    key_valid = jnp.concatenate([image_valid, text_valid])
    sequence = jnp.concatenate([image_part, prompt_text], axis=0)
    normed = normalize(sequence, norm_gain).astype(jnp.bfloat16)
    length = sequence.shape[0]
    kv_width = w_kv.shape[1]

    def add_rows(shard_rows):
        return jnp.dot(normed, shard_rows, preferred_element_type=jnp.float32)

    halfway = kv_width // 2
    key_proj = add_rows(lax.all_gather(w_kv[:, :halfway], "role", axis=0, tiled=True))
    value_proj = add_rows(lax.all_gather(w_kv[:, halfway:], "role", axis=0, tiled=True))
    projected = jnp.concatenate([key_proj, value_proj], axis=1)
    quantized, scales = quantize(projected)
    blocks = length // BLK
    per_rank = blocks // rank_count + 1
    block_target = block_dest[:, 0]
    chosen_block = (block_target[:, None] == jnp.arange(rank_count)[None, :]).astype(jnp.int32)
    before_block = jnp.sum((jnp.cumsum(chosen_block, axis=0) - chosen_block) * chosen_block, axis=1)
    page_of = block_target * per_rank + before_block
    routing = (page_of[None, :] == jnp.arange(rank_count * per_rank)[:, None]).astype(jnp.bfloat16)
    send_quant = jnp.dot(
        routing, quantized.reshape(blocks, BLK * kv_width), preferred_element_type=jnp.float32
    )
    send_quant = send_quant.astype(jnp.bfloat16).reshape(rank_count, per_rank, BLK, kv_width)
    send_scale = (
        jnp.dot(routing, scales, preferred_element_type=jnp.float32)
        .astype(jnp.bfloat16)
        .reshape(rank_count, per_rank, 2 * KVH)
    )
    send_valid = jnp.dot(
        routing,
        key_valid.reshape(blocks, BLK).astype(jnp.bfloat16),
        preferred_element_type=jnp.float32,
    )
    send_valid = send_valid.astype(jnp.bfloat16).reshape(rank_count, per_rank, BLK)
    kv_cache, cache_scale, cache_valid = (
        lax.all_to_all(send_quant, "role", split_axis=0, concat_axis=0, tiled=True),
        lax.all_to_all(send_scale, "role", split_axis=0, concat_axis=0, tiled=True),
        lax.all_to_all(send_valid, "role", split_axis=0, concat_axis=0, tiled=True),
    )
    every_query = lax.all_gather(new_query, "role", axis=0, tiled=True)
    stacked = kv_cache.astype(jnp.float32).reshape(rank_count, per_rank, BLK, 2, KVH, HD)
    stacked = stacked * cache_scale.astype(jnp.float32).reshape(rank_count, per_rank, 1, 2, KVH, 1)
    grouped = every_query.astype(jnp.float32).reshape(rank_count, KVH, groups, HD)
    scores = (
        jnp.einsum("scbkd,skgd->skgcb", stacked[:, :, :, 0], grouped, precision=highest_prec)
        * factor
    )
    present = cache_valid.astype(jnp.float32)[:, None, None] > 0.5
    scores = jnp.where(present, scores, -1e30)
    highest = jnp.max(scores, axis=(3, 4))
    weights = jnp.where(present, jnp.exp(scores - highest[..., None, None]), 0.0)
    total_sum = jnp.sum(weights, axis=(3, 4))
    summed = jnp.einsum("skgcb,scbkd->skgd", weights, stacked[:, :, :, 1], precision=highest_prec)
    past_pages = past_cache.shape[0]
    owner_hot = past_owner[:, 0][:, None] == jnp.arange(rank_count)[None, :]
    owner_weight = owner_hot.astype(jnp.float32)
    past_stack = past_cache.astype(jnp.float32).reshape(past_pages, BLK, 2, KVH, HD)
    past_stack = past_stack * past_scale.astype(jnp.float32).reshape(past_pages, 1, 2, KVH, 1)
    page_query = jnp.einsum("pr,rkgd->pkgd", owner_weight, grouped, precision=highest_prec)
    page_scores = (
        jnp.einsum("pbkd,pkgd->pkgb", past_stack[:, :, 0], page_query, precision=highest_prec)
        * factor
    )
    page_top = jnp.max(page_scores, axis=3)
    page_weights = jnp.exp(page_scores - page_top[..., None])
    page_sum_w = jnp.sum(page_weights, axis=3)
    page_summed = jnp.einsum(
        "pkgb,pbkd->pkgd", page_weights, past_stack[:, :, 1], precision=highest_prec
    )
    owned_mask = owner_hot[:, :, None, None]
    masked_top = jnp.where(owned_mask, page_top[:, None], -1e30)
    past_top = jnp.max(masked_top, axis=0)
    page_factor = jnp.where(owned_mask, jnp.exp(masked_top - past_top[None]), 0.0)
    past_total = jnp.sum(page_factor * page_sum_w[:, None], axis=0)
    past_summed = jnp.einsum("prkg,pkgd->rkgd", page_factor, page_summed, precision=highest_prec)
    highest, total_sum, summed = combine(
        (highest, total_sum, summed), (past_top, past_total, past_summed)
    )
    all_top, all_total, all_summed = joined((highest, total_sum, summed), "role", combine)
    run_top = lax.dynamic_index_in_dim(all_top, myself, 0, keepdims=False)
    run_total = lax.dynamic_index_in_dim(all_total, myself, 0, keepdims=False)
    run_summed = lax.dynamic_index_in_dim(all_summed, myself, 0, keepdims=False)
    fresh_vals = new_kv[0].astype(jnp.float32).reshape(2, KVH, HD)
    own_query = new_query[0].astype(jnp.float32).reshape(KVH, groups, HD)
    own_score = jnp.einsum("kd,kgd->kg", fresh_vals[0], own_query, precision=highest_prec) * factor
    final_top = jnp.maximum(run_top, own_score)
    old_factor = jnp.exp(run_top - final_top)
    own_weight = jnp.exp(own_score - final_top)
    final_total = run_total * old_factor + own_weight
    final_summed = (
        run_summed * old_factor[..., None] + own_weight[..., None] * fresh_vals[1][:, None, :]
    )
    attended = (final_summed / final_total[..., None]).reshape(1, H * HD).astype(jnp.bfloat16)
    return (
        kv_cache.reshape(rank_count * per_rank, BLK, kv_width),
        cache_scale.reshape(rank_count * per_rank, 2 * KVH),
        attended,
    )


def solution(mesh):
    in_specs = (
        P(("outer", "role"), None),
        P(),
        P(None, "role"),
        P(("outer", "role"), None),
        P(),
        P("role", None),
        P(("outer", "role"), None),
        P(("outer", "role"), None),
        P(("outer", "role")),
        P(("outer", "role")),
        P(("outer", "role"), None),
        P(("outer", "role"), None),
        P(("outer", "role"), None, None),
        P(("outer", "role"), None),
        P(("outer", "role"), None),
    )
    out_specs = (
        P(("outer", "role"), None, None),
        P(("outer", "role"), None),
        P(("outer", "role"), None),
    )
    return jax.shard_map(body, mesh=mesh, in_specs=in_specs, out_specs=out_specs, check_vma=False)
```

profile of v0, /device:TPU:0, one launch (start us, length us, event | category | flops | bytes accessed | tf_op | source)
XLA Modules:
  0.0 586.3 jit_solution(17531540392338131048)
XLA Ops:
  8.0 3.0 fusion.81
  13.4 13.7 %all-reduce.2 = (s32[32]{0:T(128)S(1)}, s32[32]{0:T(128)S(1)}) all-reduce(s32[32]{0:T(128)S(1)} %bitcast_dynamic-update-slice_fusion, s32[32]{0:T(128)S(1)} %dynamic-update-slice.1), channel_id=2, replica_groups=mesh['outer'=2,'role'=16] {'role'}, use_global_device_ids=true, to_apply=%add | all-reduce | flops 64 | bytes 512 | tf_op jit(solution)/shard_map/all_gather | solution.py:103
  28.8 27.5 %all-gather.8.cloned.1.call-done = bf16[256,5120]{1,0:T(8,128)(2,1)} async-done(((bf16[16,5120]{1,0:T(8,128)(2,1)}), bf16[256,5120]{1,0:T(8,128)(2,1)}) %all-gather.8.cloned.1.call-update) | async-done | bytes 2621456 | tf_op jit(solution)/shard_map/all_gather | solution.py:97
  56.3 2.3 fusion.6
  58.6 4.9 fusion.24
  64.9 3.6 all-to-all-start
  70.2 21.4 %all-to-all-done = bf16[16,32,512]{2,1,0:T(8,128)(2,1)S(1)} async-done(((bf16[16,32,512]{2,1,0:T(8,128)(2,1)}), bf16[16,32,512]{2,1,0:T(8,128)(2,1)S(1)}, u32[]{:S(2)}, u32[]{:S(2)}) %all-to-all-start) | async-done | bytes 524320 | tf_op jit(solution)/shard_map/all_to_all | solution.py:114
  91.5 10.0 %all-to-all-start.3 = ((bf16[16,2,16]{2,1,0:T(2,128)(2,1)}), bf16[16,2,16]{2,1,0:T(2,128)(2,1)S(1)}, u32[]{:S(2)}, u32[]{:S(2)}) async-start(bf16[16,2,16]{2,1,0:T(2,128)(2,1)} %bitcast.15), calls=%async_computation.3 | async-start | bytes 16384 | tf_op jit(solution)/shard_map/all_to_all | solution.py:159
  101.6 3.1 fusion.3
  104.7 91.1 %all-gather.10.cloned.1.call-done = bf16[8192,1024]{1,0:T(8,128)(2,1)} async-done(((bf16[512,1024]{1,0:T(8,128)(2,1)}), bf16[8192,1024]{1,0:T(8,128)(2,1)}) %all-gather.10.cloned.1.call-update) | async-done | bytes 16777232 | tf_op jit(solution)/shard_map/all_gather | solution.py:130
  195.8 9.6 %convolution_bitcast_fusion.1 = f32[34,8,8,128]{3,1,2,0:T(8,128)S(1)} fusion(bf16[8192,1024]{1,0:T(8,128)(2,1)} %all-gather.10.cloned.1.call-done, f32[8192]{0:T(1024)S(1)} %copy-done.15, f32[272]{0:T(512)S(1)} %add_rsqrt_fusion, bf16[240,8192]{1,0:T(8,128)(2,1)} %param.20, bf16[32,8192]{1,0:T(8,128)(2,1)S(1)} %bitcast.214), kind=kOutput, calls=%fused_computation.38 | convolution fusion | flops 4579000320 | bytes 22381632 | tf_op jit(solution)/shard_map/dot_general | solution.py:127
  205.6 117.4 %all-gather.12.cloned.1.call-done = bf16[8192,1024]{1,0:T(8,128)(2,1)} async-done(((bf16[512,1024]{1,0:T(8,128)(2,1)}), bf16[8192,1024]{1,0:T(8,128)(2,1)}) %all-gather.12.cloned.1.call-update) | async-done | bytes 16777232 | tf_op jit(solution)/shard_map/all_gather | solution.py:131
  323.0 9.7 %convolution_bitcast_fusion = f32[34,8,8,128]{3,1,2,0:T(8,128)S(1)} fusion(bf16[8192,1024]{1,0:T(8,128)(2,1)} %all-gather.12.cloned.1.call-done, f32[8192]{0:T(1024)S(1)} %copy-done.15, f32[272]{0:T(512)S(1)} %add_rsqrt_fusion, bf16[240,8192]{1,0:T(8,128)(2,1)} %param.20, bf16[32,8192]{1,0:T(8,128)(2,1)S(1)} %bitcast.215), kind=kOutput, calls=%fused_computation.37 | convolution fusion | flops 4579000320 | bytes 22381632 | tf_op jit(solution)/shard_map/dot_general | solution.py:127
  336.6 3.5 all-to-all-start.2
  340.8 2.5 copy.248
  343.3 3.1 all-to-all-done.2
  346.4 3.7 all-to-all-start.1
  350.2 56.5 %all-gather.2 = bf16[16,1,8192]{2,1,0:T(2,128)(2,1)S(1)} all-gather(bf16[1,1,8192]{2,1,0:T(2,128)(2,1)S(1)} %bitcast.219), channel_id=1, replica_groups=mesh['outer'=2,'role'=16] {'role'}, dimensions={0}, use_global_device_ids=true | all-gather | bytes 278528 | tf_op jit(solution)/shard_map/all_gather | solution.py:161
  406.7 1.5 reduce
  408.3 4.1 copy.252
  412.9 3.5 copy_multiply_fusion
  416.4 1.9 copy-done.1
  418.3 4.0 fusion.82
  424.1 3.7 fusion.13
  427.8 2.5 fusion.27
  433.0 1.5 copy.218
  436.8 1.9 copy-done
  438.7 9.3 %fusion.83 = (f32[16,8,8]{2,1,0:T(8,128)}, f32[16,8,8,2,16]{4,2,3,1,0:T(8,128)}) fusion(bf16[16,8,8,128,1]{3,2,1,0,4:T(8,128)(2,1)S(1)} %bitcast.210, f32[16,2,16,2,8,128]{5,2,1,4,0,3:T(8,128)S(1)} %copy_multiply_fusion.1, pred[16,2,16]{2,1,0:T(4,128)(4,1)S(1)} %convert_compare_fusion), kind=kOutput, calls=%fused_computation.148 | convolution fusion | flops 50428928 | bytes 2502656 | tf_op jit(solution)/shard_map/scbkd,skgd->skgcb/dot_general | solution.py:166
  451.3 5.1 fusion.23
  457.2 1.4 reduce.2
  462.8 1.6 fusion.31
  465.5 27.0 %all_gather.39 = f32[16,16,8,8]{1,3,2,0:T(8,128)S(1)} all-gather(f32[1,16,8,8]{1,3,2,0:T(8,128)S(1)} %copy.229), channel_id=1, replica_groups=mesh['outer'=2,'role'=16] {'role'}, dimensions={0}, use_global_device_ids=true | all-gather | bytes 69632 | tf_op jit(solution)/shard_map/all_gather | solution.py:17
  492.4 20.8 %all_gather.38 = f32[16,16,8,8]{1,3,2,0:T(8,128)S(1)} all-gather(f32[1,16,8,8]{1,3,2,0:T(8,128)S(1)} %copy.226), channel_id=1, replica_groups=mesh['outer'=2,'role'=16] {'role'}, dimensions={0}, use_global_device_ids=true | all-gather | bytes 69632 | tf_op jit(solution)/shard_map/all_gather | solution.py:17
  514.1 25.0 %all-gather.14.cloned.1.call-done = f32[256,8,8,128]{3,2,1,0:T(8,128)} async-done(((f32[16,8,8,128]{3,2,1,0:T(8,128)}), f32[256,8,8,128]{3,2,1,0:T(8,128)}) %all-gather.14.cloned.1.call-update) | async-done | bytes 8388624 | tf_op jit(solution)/shard_map/all_gather | solution.py:17
  540.1 36.7 %while.19 = (s32[]{:T(128)}, f32[16,8,8]{0,2,1:T(8,128)S(1)}, f32[16,8,8]{0,2,1:T(8,128)S(1)}, f32[16,8,8,128]{3,2,1,0:T(8,128)S(1)}, f32[16,16,8,8]{1,3,2,0:T(8...) while((s32[]{:T(128)}, f32[16,8,8]{0,2,1:T(8,128)S(1)}, ...), condition=%wide.region_15.16_spmd, body=%wide.region_14.15_spmd.sunk | while | flops 399365 | bytes 1630359 | solution.py:22
  541.1 1.4 fusion.93
  543.6 1.4 fusion.93
  546.0 1.4 fusion.93
  548.5 1.4 fusion.93
  550.9 1.4 fusion.93
  553.4 1.4 fusion.93
  555.8 1.4 fusion.93
  558.3 1.4 fusion.93
  560.7 1.4 fusion.93
  563.2 1.4 fusion.93
  565.6 1.4 fusion.93
  568.0 1.4 fusion.93
  570.5 1.4 fusion.93
  (179 shorter events, 49.6 us)
Async XLA Ops:
  7.2 4.6 copy-start.19
  7.2 5.9 %copy-start.17 = (s32[2]{0:T(128)S(1)}, s32[2]{0:T(128)}, u32[]{:S(2)}) copy-start(s32[2]{0:T(128)} %param.26) | copy-start | bytes 28
  7.2 6.1 %copy-start.18 = (s32[2,1]{0,1:T(1,128)S(1)}, s32[2,1]{0,1:T(1,128)}, u32[]{:S(2)}) copy-start(s32[2,1]{0,1:T(1,128)} %param.27) | copy-start | bytes 28
  7.2 21.5 %copy-start.14 = (s32[17,1]{0,1:T(1,128)S(1)}, s32[17,1]{0,1:T(1,128)}, u32[]{:S(2)}) copy-start(s32[17,1]{0,1:T(1,128)} %param.28) | copy-start | bytes 208
  7.2 49.1 %all-gather.8.cloned.1.call-start = ((), (), s32[]{:S(2)}) async-start(), calls=%async_computation.4 | async-start | bytes 2785280 | tf_op jit(solution)/shard_map/all_gather | solution.py:97
  7.9 50.7 %copy-start.16 = (f32[5120]{0:T(1024)S(1)}, f32[5120]{0:T(1024)}, u32[]{:S(2)}) copy-start(f32[5120]{0:T(1024)} %param.18) | copy-start | bytes 61444
  8.0 187.9 %all-gather.10.cloned.1.call-start = ((), (), s32[]{:S(2)}) async-start(), calls=%async_computation.5 | async-start | bytes 17825792 | tf_op jit(solution)/shard_map/all_gather | solution.py:130
  11.1 312.0 %all-gather.12.cloned.1.call-start = ((), (), s32[]{:S(2)}) async-start(), calls=%async_computation.6 | async-start | bytes 17825792 | tf_op jit(solution)/shard_map/all_gather | solution.py:131
  63.6 132.2 %copy-start.15 = (f32[8192]{0:T(1024)S(1)}, f32[8192]{0:T(1024)}, u32[]{:S(2)}) copy-start(f32[8192]{0:T(1024)} %param.21) | copy-start | bytes 98308
  64.9 26.6 %all-to-all-start = ((bf16[16,32,512]{2,1,0:T(8,128)(2,1)}), bf16[16,32,512]{2,1,0:T(8,128)(2,1)S(1)}, u32[]{:S(2)}, u32[]{:S(2)}) async-start(bf16[16,32,512]{2,1,0:T(8,128)(2,1)} %reshape.353), calls=%async_computation | async-start | bytes 1048576 | tf_op jit(solution)/shard_map/all_to_all | solution.py:114
  91.5 245.1 %all-to-all-start.3 = ((bf16[16,2,16]{2,1,0:T(2,128)(2,1)}), bf16[16,2,16]{2,1,0:T(2,128)(2,1)S(1)}, u32[]{:S(2)}, u32[]{:S(2)}) async-start(bf16[16,2,16]{2,1,0:T(2,128)(2,1)} %bitcast.15), calls=%async_computation.3 | async-start | bytes 16384 | tf_op jit(solution)/shard_map/all_to_all | solution.py:159
  336.6 9.8 %copy-start.11 = (bf16[16,2,16]{2,1,0:T(2,128)(2,1)}, bf16[16,2,16]{2,1,0:T(2,128)(2,1)S(1)}, u32[]{:S(2)}) copy-start(bf16[16,2,16]{2,1,0:T(2,128)(2,1)S(1)} %all-to-all-done.3) | copy-start | bytes 3076
  336.6 9.8 %all-to-all-start.2 = ((bf16[16,2,16]{2,1,0:T(2,128)(2,1)}), bf16[16,2,16]{2,1,0:T(2,128)(2,1)S(1)}, u32[]{:S(2)}, u32[]{:S(2)}) async-start(bf16[16,2,16]{2,1,0:T(2,128)(2,1)} %bitcast.12), calls=%async_computation.2 | async-start | bytes 16384 | tf_op jit(solution)/shard_map/all_to_all | solution.py:158
  340.8 9.4 %copy-start.9 = (bf16[1,8192]{1,0:T(2,128)(2,1)S(1)}, bf16[1,8192]{1,0:T(2,128)(2,1)}, u32[]{:S(2)}) copy-start(bf16[1,8192]{1,0:T(2,128)(2,1)} %param.23) | copy-start | bytes 49156
  346.4 88.1 %all-to-all-start.1 = ((bf16[16,2,16,2048]{3,2,1,0:T(8,128)(2,1)}), bf16[16,2,16,2048]{3,2,1,0:T(8,128)(2,1)S(1)}, u32[]{:S(2)}, u32[]{:S(2)}) async-start(bf16[16,2,16,2048]{3,2,1,0:T(8,128)(2,1)} %bitcast.204), calls=%async_computation.1 | async-start | bytes 4194304 | tf_op jit(solution)/shard_map/all_to_all | solution.py:157
  350.1 62.3 %copy-start.12 = (bf16[32,16]{0,1:T(8,128)(2,1)S(1)}, bf16[32,16]{0,1:T(8,128)(2,1)}, u32[]{:S(2)}) copy-start(bf16[32,16]{0,1:T(8,128)(2,1)} %param.30) | copy-start | bytes 3076
  350.2 62.4 %copy-start.13 = (s32[32,1]{0,1:T(1,128)S(1)}, s32[32,1]{0,1:T(1,128)}, u32[]{:S(2)}) copy-start(s32[32,1]{0,1:T(1,128)} %param.31) | copy-start | bytes 388
  350.2 188.9 %all-gather.14.cloned.1.call-start = ((), (), s32[]{:S(2)}) async-start(), calls=%async_computation.7 | async-start | bytes 8912896 | tf_op jit(solution)/shard_map/all_gather | solution.py:17
  416.4 1.9 copy-start.1
  423.1 4.7 copy-start.7
  423.1 4.7 copy-start.10
  424.1 6.1 %copy-start.4 = (f32[16,8,8]{0,2,1:T(8,128)}, f32[16,8,8]{0,2,1:T(8,128)S(1)}, u32[]{:S(2)}) copy-start(f32[16,8,8]{0,2,1:T(8,128)S(1)} %select_reduce_fusion) | copy-start | bytes 12292
  434.5 0.9 copy-start.6
  436.8 1.9 copy-start
  448.0 8.5 %copy-start.5 = (f32[16,8,8]{0,2,1:T(8,128)S(1)}, f32[16,8,8]{0,2,1:T(8,128)}, u32[]{:S(2)}) copy-start(f32[16,8,8]{0,2,1:T(8,128)} %copy-done.4) | copy-start | bytes 12292
  448.0 11.4 %copy-start.8 = (f32[32,8,8]{0,2,1:T(8,128)S(1)}, f32[32,8,8]{0,2,1:T(8,128)}, u32[]{:S(2)}) copy-start(f32[32,8,8]{0,2,1:T(8,128)} %copy.224) | copy-start | bytes 24580
  448.0 14.8 %copy-start.2 = (f32[16,8,8]{2,1,0:T(8,128)S(1)}, f32[16,8,8]{2,1,0:T(8,128)}, u32[]{:S(2)}) copy-start(f32[16,8,8]{2,1,0:T(8,128)} %get-tuple-element.243) | copy-start | bytes 12292
  513.3 0.8 copy-start.3
Sparse Core Ops, SparseCore 0:
  10.3 45.8 all-gather.7
  59.0 136.7 all-gather.9
  198.0 125.0 all-gather.11
  456.6 82.4 all-gather.13
where the time goes:
time: 593 us; the launch traced here: 586 us
  waiting for transfers between devices  287 us (48%)
  blocking collectives  118 us (20%)
  other arithmetic  59.4 us (10%)
  matrix products  51.1 us (9%)
  local copies, waits for them, and re-layouts  33.5 us (6%)
  starting transfers between devices  20.9 us (4%)
  between operations  16 us (3%)
    all_gather x1, waiting for transfers between devices, body(): lax.all_gather(w_kv[:, halfway:], 'role', axis=0, tiled=True)  117 us
    all_gather x1, waiting for transfers between devices, body(): lax.all_gather(w_kv[:, :halfway], 'role', axis=0, tiled=True)  91.1 us
    all_gather x1, blocking collectives, body(): every_query = lax.all_gather(new_query, 'role', axis=0, tiled=True)  56.5 us
    all_gather x2, blocking collectives, joined(): gathered = jax.tree.map(lambda a: lax.all_gather(a, axis), part)  47.8 us
    all_gather x1, waiting for transfers between devices, body(): lax.all_gather(images, 'role', axis=0, tiled=True)  27.5 us
    all_gather x1, waiting for transfers between devices, joined(): gathered = jax.tree.map(lambda a: lax.all_gather(a, axis), part)  25 us
    add x15, other arithmetic, combine(): left_summed * left_factor[..., None]  21.6 us
    all_to_all x1, waiting for transfers between devices, body(): lax.all_to_all(outgoing, 'role', split_axis=0, concat_axis=2, tiled=True)  21.4 us
  transfers between devices with their start and end apart: 8, of which 6 were waited for; matrix products, arithmetic and copies ran while one was open for 14% of the time, Pallas kernels for 0%

commit v1 on v0

v1 whole, which is shorter than its diff:
```python
import functools
import math

import jax
import jax.numpy as jnp
from jax import lax
from jax.experimental import pallas as pl
from jax.experimental.pallas import tpu as pltpu
from jax.sharding import PartitionSpec as P

H = 64
KVH = 8
HD = 128
IMG_TOK = 8
IMGCAP = 4
BLK = 16


MESH = pl.DeviceIdType.MESH
CHUNK = 512


def normalize(values, gain_vec):
    values = values.astype(jnp.float32)
    return values * lax.rsqrt(jnp.mean(values * values, axis=-1, keepdims=True) + 1e-06) * gain_vec


def rotate(key_part):
    halfway = HD // 2
    position = jnp.arange(key_part.shape[0]).astype(jnp.float32)
    inverse = jnp.exp(jnp.arange(halfway).astype(jnp.float32) * (-2.0 * math.log(1000000.0) / HD))
    angles = position[:, None] * inverse[None, :]
    cosine = jnp.cos(angles)[:, None, :]
    sine_part = jnp.sin(angles)[:, None, :]
    front_half = key_part[..., :halfway]
    back_half = key_part[..., halfway:]
    return jnp.concatenate(
        [front_half * cosine - back_half * sine_part, back_half * cosine + front_half * sine_part],
        axis=-1,
    )


def quantize(projected):
    length = projected.shape[0]
    key_part = rotate(projected[:, : KVH * HD].reshape(length, KVH, HD))
    value_part = projected[:, KVH * HD :].reshape(length, KVH, HD)
    stacked = jnp.stack([key_part, value_part], axis=1).reshape(length // BLK, BLK, 2, KVH, HD)
    largest = jnp.max(jnp.abs(stacked), axis=(1, 4))
    scales = ((largest + 1e-05) / 448.0).astype(jnp.bfloat16)
    quantized = (stacked / scales.astype(jnp.float32)[:, None, :, :, None]).astype(jnp.bfloat16)
    return (
        quantized.reshape(length // BLK, BLK, 2 * KVH * HD),
        scales.reshape(length // BLK, 2 * KVH),
    )


def combine(earlier, later):
    left_top, left_total, left_summed = earlier
    right_top, right_total, right_summed = later
    highest = jnp.maximum(left_top, right_top)
    left_factor = jnp.exp(left_top - highest)
    right_factor = jnp.exp(right_top - highest)
    return (
        highest,
        left_total * left_factor + right_total * right_factor,
        left_summed * left_factor[..., None] + right_summed * right_factor[..., None],
    )


def front_kernel(
    n, payload, vis_gain, w_merge, text, norm_gain, w_kv,
    projected, extras,
    ibuf, wm, nimg, mout, mbuf, abuf, arecv, wq, csend, crecv,
    img_s, img_r, sib_s, sib_r, mrg_s, mrg_r, at_s, at_r, ai_s, ai_r,
    z_s, z_r, ws_s, ws_r, c_s, c_r, loc,
):
    nz = n // 4
    chips = n // 2
    vis = vis_gain.shape[1]
    x = lax.axis_index("outer")
    r = lax.axis_index("role")
    z = r // 4
    y = (r // 2) % 2
    c = r % 2
    q = r // 2
    sib = q * 2 + (1 - c)
    width = w_merge.shape[1]
    half = width // 2
    rows_t = text.shape[0]
    rows_i = IMGCAP * IMG_TOK
    mine = y * 2 + x

    def rdma(src, dst, ss, rs, outer, role):
        return pltpu.make_async_remote_copy(
            src_ref=src, dst_ref=dst, send_sem=ss, recv_sem=rs,
            device_id=(outer, role), device_id_type=MESH,
        )

    def member(d):
        dx, dy = d % 2, d // 2
        ox, oy = (x + dx) % 2, (y + dy) % 2
        return oy * 2 + ox, ox, z * 4 + oy * 2 + c

    barrier = pltpu.get_barrier_semaphore()
    for k in range(1, n):
        pl.semaphore_signal(barrier, inc=1, device_id=(x, (r + k) % n), device_id_type=MESH)
    for d in (1, 3):
        _, ox, role = member(d)
        pl.semaphore_signal(barrier, inc=1, device_id=(ox, role), device_id_type=MESH)
    wm_copy = pltpu.make_async_copy(w_merge, wm, loc.at[0])
    wm_copy.start()
    pl.semaphore_wait(barrier, n + 1)

    def img_copy(k):
        slot = ibuf.at[r]
        return rdma(payload, slot, img_s.at[k], img_r.at[k], x, ((q + k) % chips) * 2 + c)

    for k in range(1, chips):
        img_copy(k).start()
    rdma(payload, ibuf.at[r], sib_s.at[0], sib_r.at[0], x, sib).start()
    own_img = pltpu.make_async_copy(payload, ibuf.at[r], loc.at[1])
    own_img.start()

    def piece(zz, core):
        return wq.at[pl.ds(pl.multiple_of((zz * 2 + core) * half, half), half), :]

    own_rows = w_kv.at[pl.ds(pl.multiple_of(x * half, half), half), :]
    own_w = pltpu.make_async_copy(own_rows, piece(z, c), loc.at[2])
    own_w.start()

    def z_copy(way, t, src, zz):
        role = ((z + (1 if way == 0 else nz - 1)) % nz) * 4 + y * 2 + c
        return rdma(src, piece(zz, c), z_s.at[way, t], z_r.at[way, t], x, role)

    def w_sib(i, src, zz):
        return rdma(src, piece(zz, c), ws_s.at[i], ws_r.at[i], x, sib)

    @pl.when(z < nz - 1)
    def _():
        z_copy(0, 1, own_rows, z).start()

    @pl.when(z > 0)
    def _():
        z_copy(1, 1, own_rows, z).start()

    w_sib(0, own_rows, z).start()

    def norm_rows(i, carry):
        at = pl.multiple_of(i * 16, 16)
        v = text[pl.ds(at, 16), :].astype(jnp.float32)
        inv = lax.rsqrt(jnp.mean(v * v, axis=1, keepdims=True) + 1e-06)
        v = (v * inv * norm_gain[...]).astype(jnp.bfloat16)
        for g in range(4):
            for s in range(chips):
                col = (s // 2) * 4 * width + (g // 2) * 2 * width + (s % 2) * width + (g % 2) * half
                abuf[g, pl.ds(rows_i + at, 16), s * half : (s + 1) * half] = v[:, col : col + half]
        return carry

    lax.fori_loop(0, rows_t // 16, norm_rows, 0)

    def a_copy(d, lo, size, ss, rs):
        g, ox, role = member(d)
        return rdma(
            abuf.at[g, pl.ds(lo, size), :], arecv.at[d - 1, pl.ds(lo, size), :],
            ss.at[d - 1], rs.at[d - 1], ox, role,
        )

    for d in range(1, 4):
        a_copy(d, rows_i, rows_t, at_s, at_r).start()

    own_img.wait()
    for k in range(1, chips):
        src = ((q + chips - k) % chips) * 2 + c
        rdma(payload, ibuf.at[src], img_s.at[k], img_r.at[k], x, sib).wait_recv()
        rdma(ibuf.at[src], ibuf.at[src], sib_s.at[k], sib_r.at[k], x, sib).start()
    for k in range(chips):
        src = ((q + chips - k) % chips) * 2 + (1 - c)
        rdma(payload, ibuf.at[src], sib_s.at[k], sib_r.at[k], x, sib).wait_recv()

    def norm_images(i, carry):
        v = ibuf[i, :, :vis].astype(jnp.float32)
        inv = lax.rsqrt(jnp.mean(v * v, axis=1, keepdims=True) + 1e-06)
        nimg[pl.ds(pl.multiple_of(i * 16, 16), 16), :] = (v * inv * vis_gain[...]).astype(jnp.bfloat16)
        extras[i, :, :] = ibuf[i, :, vis:]
        return carry

    lax.fori_loop(0, n, norm_images, 0)
    wm_copy.wait()
    merged = jnp.dot(nimg[...], wm[...], preferred_element_type=jnp.float32).astype(jnp.bfloat16)

    images = 2 * n
    lane = lax.broadcasted_iota(jnp.int32, (1, images * IMG_TOK), 1)
    image = lane // IMG_TOK
    last = ibuf.shape[2]
    named = [
        jnp.concatenate(
            [ibuf[i // 2, i % 2 : i % 2 + 1, last - 128 :].astype(jnp.float32)] * (images * IMG_TOK // 128), axis=1
        )
        for i in range(images)
    ]
    target = jnp.zeros(lane.shape, jnp.float32)
    for i in range(images):
        target = jnp.where(image == i, named[i], target)
    place = target * float(IMGCAP)
    for i in range(images):
        place = place + jnp.where((image > i) & (named[i] == target), 1.0, 0.0)
    row = lax.broadcasted_iota(jnp.int32, (n * rows_i, images * IMG_TOK), 0)
    col = lax.broadcasted_iota(jnp.int32, (n * rows_i, images * IMG_TOK), 1)
    hot = ((row // IMG_TOK).astype(jnp.float32) == place) & (row % IMG_TOK == col % IMG_TOK)
    placed = jnp.dot(
        jnp.where(hot, 1.0, 0.0).astype(jnp.bfloat16), merged, preferred_element_type=jnp.float32
    ).astype(jnp.bfloat16)
    for p in range(n):
        mout[p] = placed[p * rows_i : (p + 1) * rows_i]
    for k in range(1, n):
        to = (r + k) % n
        rdma(mout.at[to], mbuf.at[r], mrg_s.at[k], mrg_r.at[k], x, to).start()
    own_m = pltpu.make_async_copy(mout.at[r], mbuf.at[r], loc.at[1])
    own_m.start()
    own_m.wait()

    def hop(t):
        @pl.when(z - t >= 0)
        def _():
            z_copy(0, t, own_rows, z - t).wait_recv()

            @pl.when(z < nz - 1)
            def _():
                z_copy(0, t + 1, piece(z - t, c), z - t).start()

            w_sib(t, piece(z - t, c), z - t).start()

        @pl.when(z + t < nz)
        def _():
            z_copy(1, t, own_rows, z + t).wait_recv()

            @pl.when(z > 0)
            def _():
                z_copy(1, t + 1, piece(z + t, c), z + t).start()

            w_sib(nz - 1 + t, piece(z + t, c), z + t).start()

    hop(1)
    for k in range(1, n):
        src = (r + n - k) % n
        rdma(mout.at[src], mbuf.at[src], mrg_s.at[k], mrg_r.at[k], x, sib).wait_recv()
    squares = jnp.zeros((rows_i, 1), jnp.float32)
    for s in range(n):
        v = mbuf[s].astype(jnp.float32)
        squares = squares + jnp.sum(v * v, axis=1, keepdims=True)
    inv = lax.rsqrt(squares / float(n * width) + 1e-06)
    for s in range(n):
        v = (mbuf[s].astype(jnp.float32) * inv * norm_gain[:, s * width : (s + 1) * width]).astype(jnp.bfloat16)
        spot = (s // 4) * 2 + s % 2
        for e in range(2):
            abuf[((s // 2) % 2) * 2 + e, 0:rows_i, spot * half : (spot + 1) * half] = v[:, e * half : (e + 1) * half]
    for d in range(1, 4):
        a_copy(d, 0, rows_i, ai_s, ai_r).start()

    for t in range(2, nz):
        hop(t)
    own_w.wait()
    w_sib(0, own_rows, z).wait_recv()
    for t in range(1, nz):
        @pl.when(z - t >= 0)
        def _():
            w_sib(t, own_rows, z - t).wait_recv()

        @pl.when(z + t < nz)
        def _():
            w_sib(nz - 1 + t, own_rows, z + t).wait_recv()

    kv_width = w_kv.shape[1]
    for d in range(1, 4):
        a_copy(d, rows_i, rows_t, at_s, at_r).wait()
        a_copy(d, 0, rows_i, ai_s, ai_r).wait()

    def c_copy(d, j):
        _, ox, role = member(d)
        return rdma(csend.at[d - 1, j], crecv.at[d - 1, j], c_s.at[d - 1, j], c_r.at[d - 1, j], ox, role)

    parts = kv_width // CHUNK

    def partials(j, carry):
        cols = pl.ds(pl.multiple_of(j * CHUNK, CHUNK), CHUNK)
        for d in (3, 1, 2):
            csend[d - 1, j] = jnp.dot(
                arecv[d - 1], wq[:, cols], preferred_element_type=jnp.float32
            ).astype(jnp.bfloat16)
            c_copy(d, j).start()
        return carry

    lax.fori_loop(0, parts, partials, 0)

    def own_partial(j, carry):
        cols = pl.ds(pl.multiple_of(j * CHUNK, CHUNK), CHUNK)
        projected[:, cols] = jnp.dot(abuf[mine], wq[:, cols], preferred_element_type=jnp.float32)
        return carry

    lax.fori_loop(0, parts, own_partial, 0)

    def add_partials(j, carry):
        cols = pl.ds(pl.multiple_of(j * CHUNK, CHUNK), CHUNK)
        for d in range(1, 4):
            c_copy(d, j).wait()
        projected[:, cols] = (
            projected[:, cols]
            + crecv[0, j].astype(jnp.float32)
            + crecv[1, j].astype(jnp.float32)
            + crecv[2, j].astype(jnp.float32)
        )
        return carry

    lax.fori_loop(0, parts, add_partials, 0)

    for k in range(1, chips):
        img_copy(k).wait_send()
    for k in range(chips):
        rdma(payload, ibuf.at[r], sib_s.at[k], sib_r.at[k], x, sib).wait_send()
    for k in range(1, n):
        rdma(mout.at[r], mbuf.at[r], mrg_s.at[k], mrg_r.at[k], x, sib).wait_send()
    w_sib(0, own_rows, z).wait_send()
    for t in range(1, nz):
        @pl.when((z - t + 1 >= 0) & (z < nz - 1))
        def _():
            z_copy(0, t, own_rows, z).wait_send()

        @pl.when((z + t - 1 < nz) & (z > 0))
        def _():
            z_copy(1, t, own_rows, z).wait_send()

        @pl.when(z - t >= 0)
        def _():
            w_sib(t, own_rows, z).wait_send()

        @pl.when(z + t < nz)
        def _():
            w_sib(nz - 1 + t, own_rows, z).wait_send()


def front(payload, vis_gain, w_merge, text, norm_gain, w_kv):
    n = lax.axis_size("role")
    nz = n // 4
    chips = n // 2
    width = w_merge.shape[1]
    vis = vis_gain.shape[0]
    model = norm_gain.shape[0]
    rows_i = IMGCAP * IMG_TOK
    length = text.shape[0] + rows_i
    kv_width = w_kv.shape[1]
    parts = kv_width // CHUNK
    bf = jnp.bfloat16
    dma = pltpu.SemaphoreType.DMA
    vmem = pl.BlockSpec(memory_space=pltpu.VMEM)
    hbm = pl.BlockSpec(memory_space=pl.ANY)
    return pl.pallas_call(
        functools.partial(front_kernel, n),
        out_shape=(
            jax.ShapeDtypeStruct((length, kv_width), jnp.float32),
            jax.ShapeDtypeStruct((n, 16, payload.shape[1] - vis), bf),
        ),
        in_specs=[hbm, vmem, hbm, vmem, vmem, hbm],
        out_specs=(vmem, vmem),
        scratch_shapes=[
            pltpu.VMEM((n,) + payload.shape, bf),
            pltpu.VMEM(w_merge.shape, bf),
            pltpu.VMEM((n * 16, vis), bf),
            pltpu.VMEM((n, rows_i, width), bf),
            pltpu.VMEM((n, rows_i, width), bf),
            pltpu.VMEM((4, length, model // 4), bf),
            pltpu.VMEM((3, length, model // 4), bf),
            pltpu.VMEM((model // 4, kv_width), bf),
            pltpu.VMEM((3, parts, length, CHUNK), bf),
            pltpu.VMEM((3, parts, length, CHUNK), bf),
            dma((chips,)), dma((chips,)), dma((chips,)), dma((chips,)),
            dma((n,)), dma((n,)), dma((3,)), dma((3,)), dma((3,)), dma((3,)),
            dma((2, nz + 1)), dma((2, nz + 1)), dma((2 * nz,)), dma((2 * nz,)),
            dma((3, parts)), dma((3, parts)), dma((3,)),
        ],
        compiler_params=pltpu.CompilerParams(
            collective_id=0, has_side_effects=True, vmem_limit_bytes=56 * 1024 * 1024
        ),
        name="front",
    )(payload, vis_gain[None, :], w_merge, text, norm_gain[None, :], w_kv)


def tail(
    projected, every_query, counts, targets,
    new_query, new_kv, text_len, block_dest, past_cache, past_scale, past_owner,
):
    rank_count = lax.axis_size("role")
    myself = lax.axis_index("role")
    groups = H // KVH
    factor = 1.0 / math.sqrt(HD)
    highest_prec = lax.Precision.HIGHEST
    bf = jnp.bfloat16
    length, kv_width = projected.shape
    chosen = (targets[:, None] == jnp.arange(rank_count)[None, :]).astype(jnp.int32)
    before = jnp.sum((jnp.cumsum(chosen, axis=0) - chosen) * chosen, axis=1)
    slot_of = targets * IMGCAP + before
    is_mine = slot_of[None, :] == myself * IMGCAP + jnp.arange(IMGCAP)[:, None]
    slot_count = jnp.sum(jnp.where(is_mine, counts[None, :], 0), axis=1)
    image_valid = (jnp.arange(IMG_TOK)[None, :] < slot_count[:, None]).reshape(-1)
    text_valid = jnp.arange(length - IMGCAP * IMG_TOK) < text_len[0]
    key_valid = jnp.concatenate([image_valid, text_valid])
    quantized, scales = quantize(projected)
    blocks = length // BLK
    per_rank = blocks // rank_count + 1
    block_target = block_dest[:, 0]
    chosen_block = (block_target[:, None] == jnp.arange(rank_count)[None, :]).astype(jnp.int32)
    before_block = jnp.sum((jnp.cumsum(chosen_block, axis=0) - chosen_block) * chosen_block, axis=1)
    page_of = block_target * per_rank + before_block
    routing = (page_of[None, :] == jnp.arange(rank_count * per_rank)[:, None]).astype(bf)
    send_quant = jnp.dot(
        routing, quantized.reshape(blocks, BLK * kv_width), preferred_element_type=jnp.float32
    )
    send_quant = send_quant.astype(bf).reshape(rank_count, per_rank, BLK, kv_width)
    small = jnp.concatenate([scales, key_valid.reshape(blocks, BLK).astype(bf)], axis=1)
    send_small = (
        jnp.dot(routing, small, preferred_element_type=jnp.float32)
        .astype(bf)
        .reshape(rank_count, per_rank, 2 * KVH + BLK)
    )
    kv_cache, got_small = (
        lax.all_to_all(send_quant, "role", split_axis=0, concat_axis=0, tiled=True),
        lax.all_to_all(send_small, "role", split_axis=0, concat_axis=0, tiled=True),
    )
    cache_scale, cache_valid = got_small[..., : 2 * KVH], got_small[..., 2 * KVH :]
    query = every_query.reshape(rank_count, KVH, groups, HD)

    past_pages = past_cache.shape[0]
    owner_hot = past_owner[:, 0][:, None] == jnp.arange(rank_count)[None, :]
    past_stack = past_cache.reshape(past_pages, BLK, 2, KVH, HD)
    past_factor = past_scale.astype(jnp.float32).reshape(past_pages, 2, KVH)[..., None, None]
    page_query = jnp.dot(
        owner_hot.astype(bf), every_query, preferred_element_type=jnp.float32
    ).astype(bf).reshape(past_pages, KVH, groups, HD)
    page_scores = (
        jnp.einsum("pbkd,pkgd->pkgb", past_stack[:, :, 0], page_query, preferred_element_type=jnp.float32)
        * past_factor[:, 0]
        * factor
    )
    page_top = jnp.max(page_scores, axis=3)
    page_weights = jnp.exp(page_scores - page_top[..., None])
    page_sum_w = jnp.sum(page_weights, axis=3)
    page_summed = jnp.einsum(
        "pkgb,pbkd->pkgd", (page_weights * past_factor[:, 1]).astype(bf), past_stack[:, :, 1],
        preferred_element_type=jnp.float32,
    )
    owned_mask = owner_hot[:, :, None, None]
    masked_top = jnp.where(owned_mask, page_top[:, None], -1e30)
    past_top = jnp.max(masked_top, axis=0)
    page_factor = jnp.where(owned_mask, jnp.exp(masked_top - past_top[None]), 0.0)
    past_total = jnp.sum(page_factor * page_sum_w[:, None], axis=0)
    past_summed = jnp.einsum("prkg,pkgd->rkgd", page_factor, page_summed, precision=highest_prec)

    stacked = kv_cache.reshape(rank_count, per_rank, BLK, 2, KVH, HD)
    in_factor = cache_scale.astype(jnp.float32).reshape(rank_count, per_rank, 2, KVH)
    key_factor = jnp.transpose(in_factor[:, :, 0], (0, 2, 1))[:, :, None, :, None]
    value_factor = jnp.transpose(in_factor[:, :, 1], (0, 2, 1))[:, :, None, :, None]
    scores = (
        jnp.einsum("scbkd,skgd->skgcb", stacked[:, :, :, 0], query, preferred_element_type=jnp.float32)
        * key_factor
        * factor
    )
    present = cache_valid.astype(jnp.float32)[:, None, None] > 0.5
    scores = jnp.where(present, scores, -1e30)
    highest = jnp.max(scores, axis=(3, 4))
    weights = jnp.where(present, jnp.exp(scores - highest[..., None, None]), 0.0)
    total_sum = jnp.sum(weights, axis=(3, 4))
    summed = jnp.einsum(
        "skgcb,scbkd->skgd", (weights * value_factor).astype(bf), stacked[:, :, :, 1],
        preferred_element_type=jnp.float32,
    )
    highest, total_sum, summed = combine(
        (highest, total_sum, summed), (past_top, past_total, past_summed)
    )
    packed = jnp.concatenate(
        [
            summed.reshape(rank_count, H, HD),
            jnp.concatenate(
                [highest.reshape(rank_count, 1, H), total_sum.reshape(rank_count, 1, H)], axis=2
            ),
        ],
        axis=1,
    )
    got = lax.all_to_all(packed, "role", split_axis=0, concat_axis=0, tiled=True)
    tops, totals, sums = got[:, H, :H], got[:, H, H : 2 * H], got[:, :H]
    fresh_vals = new_kv[0].astype(jnp.float32).reshape(2, KVH, HD)
    own_query = new_query[0].astype(jnp.float32).reshape(KVH, groups, HD)
    own_score = (jnp.sum(fresh_vals[0][:, None] * own_query, axis=2) * factor).reshape(H)
    final_top = jnp.maximum(jnp.max(tops, axis=0), own_score)
    old_factor = jnp.exp(tops - final_top)
    own_weight = jnp.exp(own_score - final_top)
    final_total = jnp.sum(totals * old_factor, axis=0) + own_weight
    own_value = jnp.repeat(fresh_vals[1], groups, axis=0)
    final_summed = jnp.sum(sums * old_factor[..., None], axis=0) + own_weight[:, None] * own_value
    attended = (final_summed / final_total[:, None]).reshape(1, H * HD).astype(bf)
    return (
        kv_cache.reshape(rank_count * per_rank, BLK, kv_width),
        cache_scale.reshape(rank_count * per_rank, 2 * KVH),
        attended,
    )


def plain_front(images, vis_gain, w_merge, prompt_text, norm_gain, w_kv, targets):
    rank_count = lax.axis_size("role")
    columns = w_merge.shape[1]
    normed_img = normalize(lax.all_gather(images, "role", axis=0, tiled=True), vis_gain).astype(
        jnp.bfloat16
    )
    merged = jnp.dot(normed_img, w_merge, preferred_element_type=jnp.float32).astype(jnp.bfloat16)
    image_total = targets.shape[0]
    chosen = (targets[:, None] == jnp.arange(rank_count)[None, :]).astype(jnp.int32)
    before = jnp.sum((jnp.cumsum(chosen, axis=0) - chosen) * chosen, axis=1)
    slot_of = targets * IMGCAP + before
    placing = (slot_of[None, :] == jnp.arange(rank_count * IMGCAP)[:, None]).astype(jnp.bfloat16)
    outgoing = jnp.dot(
        placing, merged.reshape(image_total, IMG_TOK * columns), preferred_element_type=jnp.float32
    )
    outgoing = outgoing.astype(jnp.bfloat16).reshape(rank_count, IMGCAP * IMG_TOK, columns)
    arrived = lax.all_to_all(outgoing, "role", split_axis=0, concat_axis=2, tiled=True)
    image_part = arrived.reshape(IMGCAP * IMG_TOK, rank_count * columns)
    sequence = jnp.concatenate([image_part, prompt_text], axis=0)
    normed = normalize(sequence, norm_gain).astype(jnp.bfloat16)
    rows = lax.all_gather(w_kv, "role", axis=0, tiled=True)
    return jnp.dot(normed, rows, preferred_element_type=jnp.float32)


def body(
    paired,
    images,
    vis_gain,
    w_merge,
    prompt_text,
    norm_gain,
    w_kv,
    new_query,
    new_kv,
    text_len,
    img_count,
    img_dest,
    block_dest,
    past_cache,
    past_scale,
    past_owner,
):
    n = lax.axis_size("role")
    if paired and images.shape[0] == 2 * IMG_TOK:
        meta = jnp.concatenate([img_dest[:, 0], img_count]).astype(jnp.bfloat16)
        meta = jnp.pad(meta, (0, 12))[:, None] * jnp.ones((1, 128), jnp.bfloat16)
        payload = jnp.concatenate([images, new_query.reshape(16, -1), meta], axis=1)
        projected, extras = front(payload, vis_gain, w_merge, prompt_text, norm_gain, w_kv)
        every_query = extras[:, :, :-128].reshape(n, -1)
        numbers = extras[:, :4, -1].astype(jnp.int32)
        targets = numbers[:, :2].reshape(-1)
        counts = numbers[:, 2:].reshape(-1)
    else:
        counts, targets = (
            lax.all_gather(img_count, "role", axis=0, tiled=True),
            lax.all_gather(img_dest[:, 0], "role", axis=0, tiled=True),
        )
        every_query = lax.all_gather(new_query, "role", axis=0, tiled=True)
        projected = plain_front(images, vis_gain, w_merge, prompt_text, norm_gain, w_kv, targets)
    return tail(
        projected, every_query, counts, targets,
        new_query, new_kv, text_len, block_dest, past_cache, past_scale, past_owner,
    )


def solution(mesh):
    in_specs = (
        P(("outer", "role"), None),
        P(),
        P(None, "role"),
        P(("outer", "role"), None),
        P(),
        P("role", None),
        P(("outer", "role"), None),
        P(("outer", "role"), None),
        P(("outer", "role")),
        P(("outer", "role")),
        P(("outer", "role"), None),
        P(("outer", "role"), None),
        P(("outer", "role"), None, None),
        P(("outer", "role"), None),
        P(("outer", "role"), None),
    )
    out_specs = (
        P(("outer", "role"), None, None),
        P(("outer", "role"), None),
        P(("outer", "role"), None),
    )
    paired = mesh.shape["outer"] == 2 and mesh.shape["role"] % 8 == 0
    return jax.shard_map(
        functools.partial(body, paired), mesh=mesh, in_specs=in_specs, out_specs=out_specs, check_vma=False
    )
```

time: 593 us -> 293 us (0.49); the launches traced: 586 us -> 292 us
  waiting for transfers between devices: 287 us -> 36.5 us
  Pallas kernels: 0 us -> 181 us
  blocking collectives: 118 us -> 0 us
  other arithmetic: 59.4 us -> 16.1 us
  matrix products: 51.1 us -> 12.1 us
  between operations: 16 us -> 1.71 us
  local copies, waits for them, and re-layouts: 33.5 us -> 25.8 us
    all_gather x4 -> x0, waiting for transfers between devices: 261 us -> none  [the longest x1 117 us: body(): lax.all_gather(w_kv[:, halfway:], 'role', axis=0, tiled=True)]
    pallas_call x0 -> x1, Pallas kernels: none -> 181 us  [front(): pl.pallas_call(functools.partial(front_kernel, n), out_shape=(jax.ShapeDt...]
    all_gather x4 -> x0, blocking collectives: 118 us -> none  [the longest x1 56.5 us: body(): every_query = lax.all_gather(new_query, 'role', axis=0, tiled=True)]
    dot_general x14 -> x8, matrix products: 51.1 us -> 12.1 us  [the longest x1 2.83 us: tail(): jnp.einsum('scbkd,skgd->skgcb', stacked[:, :, :, 0], query, preferred_ele...]
    add x35 -> x4, other arithmetic: 34.5 us -> 0.68 us  [the longest x1 0.66 us: tail(): page_of = block_target * per_rank + before_block]
    all_to_all x4 -> x3, waiting for transfers between devices: 24.5 us -> 36.5 us  [the longest x1 20.3 us: tail(): lax.all_to_all(send_quant, 'role', split_axis=0, concat_axis=0, tiled=True)]
    mul x6 -> x1, other arithmetic: 6.28 us -> 0.01 us  [tail(): jnp.sum(fresh_vals[0][:, None] * own_query, axis=2) * factor]
    all_to_all x4 -> x3, starting transfers between devices: 20.8 us -> 19.3 us  [the longest x1 11.2 us: tail(): lax.all_to_all(packed, 'role', split_axis=0, concat_axis=0, tiled=True)]
  transfers between devices with their start and end apart: 8 -> 3, of which waited for: 6 -> 3; matrix products, arithmetic and copies ran while one was open for 14% -> 9% of each run, Pallas kernels for 0% -> 0%
where the time goes in v1:
time: 293 us; the launch traced here: 292 us
  Pallas kernels  181 us (62%)
  waiting for transfers between devices  36.5 us (12%)
  local copies, waits for them, and re-layouts  25.8 us (9%)
  starting transfers between devices  19.3 us (7%)
  other arithmetic  16.1 us (5%)
  matrix products  12.1 us (4%)
    pallas_call x1, Pallas kernels, front(): pl.pallas_call(functools.partial(front_kernel, n), out_shape=(jax.ShapeDt...  181 us
    all_to_all x1, waiting for transfers between devices, tail(): lax.all_to_all(send_quant, 'role', split_axis=0, concat_axis=0, tiled=True)  20.3 us
    unnamed x39, local copies, waits for them, and re-layouts  18 us
    all_to_all x1, waiting for transfers between devices, tail(): lax.all_to_all(packed, 'role', split_axis=0, concat_axis=0, tiled=True)  14.7 us
    all_to_all x1, starting transfers between devices, tail(): lax.all_to_all(packed, 'role', split_axis=0, concat_axis=0, tiled=True)  11.2 us
  transfers between devices with their start and end apart: 3, of which 3 were waited for; matrix products, arithmetic and copies ran while one was open for 9% of the time, Pallas kernels for 0%

profile of v1, /device:TPU:0, one launch (start us, length us, event | category | flops | bytes accessed | tf_op | source)
XLA Modules:
  0.0 292.3 jit_solution(939123121614280534)
XLA Ops:
  1.3 0.7 convert.17
  2.0 0.7 convert_bitcast_fusion
  2.7 0.7 fusion.37
  3.4 0.8 select_reduce_fusion.2
  4.3 0.7 multiply_add_fusion.2
  4.9 1.5 fusion.54
  6.6 1.6 pad_maximum_fusion.3.payload
  8.2 180.8 %front.1 = (f32[272,2048]{1,0:T(8,128)}, bf16[16,16,640]{2,1,0:T(8,128)(2,1)}) custom-call(bf16[16,5760]{1,0:T(8,128)(2,1)} %pad_maximum_fusion.3.payload, f32[1,5120]{1,0:T(1,128)} %bitcast.172, bf16[5120,512]{1,0:T(8,128)(2,1)} %w_merge.1, bf16[240,8192]{1,0:T(8,128)(2,1)} %text.1, f32[1,8192]{1,0:T(1,128)} %bitcast.170, bf16[512,2048]{1,0:T(8,128)(2,1)} %w_kv.1), custom_call_target="tpu_custom_call" | custom-call | tf_op jit(solution)/shard_map/front/pallas_call | solution.py:356
  189.1 2.8 slice_bitcast_fusion.1
  192.1 0.8 copy-done.4
  194.3 1.5 copy.184
  195.8 0.6 multiply_cosine_fusion
  196.3 0.6 multiply_subtract_fusion
  196.9 0.4 pad_maximum_fusion.1
  197.6 0.7 convolution_convert_fusion.2
  198.3 3.5 %all-to-all-start.1 = ((bf16[16,2,32]{2,1,0:T(2,128)(2,1)}), bf16[16,2,32]{2,1,0:T(2,128)(2,1)S(1)}, u32[]{:S(2)}, u32[]{:S(2)}) async-start(bf16[16,2,32]{2,1,0:T(2,128)(2,1)} %bitcast.10), calls=%async_computation.1 | async-start | bytes 16384 | tf_op jit(solution)/shard_map/all_to_all | solution.py:426
  202.4 1.0 copy.185
  203.4 0.7 convolution_convert_fusion
  204.2 2.5 copy.186
  206.7 1.6 all-to-all-done.1
  208.2 4.6 %all-to-all-start = ((bf16[16,2,16,2048]{3,2,1,0:T(8,128)(2,1)}), bf16[16,2,16,2048]{3,2,1,0:T(8,128)(2,1)S(1)}, u32[]{:S(2)}, u32[]{:S(2)}) async-start(bf16[16,2,16,2048]{3,2,1,0:T(8,128)(2,1)} %bitcast.148), calls=%async_computation | async-start | bytes 4194304 | tf_op jit(solution)/shard_map/all_to_all | solution.py:425
  212.8 0.7 copy.180
  213.5 0.7 copy.179
  214.2 3.6 %copy.190 = bf16[64,8,16,128]{3,2,1,0:T(8,128)(2,1)} copy(bf16[64,8,16,128]{3,1,2,0:T(8,128)(2,1)} %bitcast.156) | data formatting | bytes 4194304
  218.1 0.3 fusion.3
  218.6 1.0 copy-done
  219.5 1.4 fusion.51
  220.9 0.8 fusion.57
  221.7 0.7 copy.158
  222.4 1.3 fusion.10
  223.7 1.6 copy.169
  225.3 1.0 select_reduce_fusion
  226.3 1.8 fusion.16
  228.1 2.0 fusion.7
  230.1 2.4 fusion.8
  232.6 0.7 copy.154
  233.6 20.3 %all-to-all-done = bf16[16,2,16,2048]{3,2,1,0:T(8,128)(2,1)S(1)} async-done(((bf16[16,2,16,2048]{3,2,1,0:T(8,128)(2,1)}), bf16[16,2,16,2048]{3,2,1,0:T(8,128)(2,1)S(1)}, u32[]{:S(2)}, u32[]{:S(2)}) %all-to-all-start) | async-done | bytes 2097184 | tf_op jit(solution)/shard_map/all_to_all | solution.py:425
  253.9 0.6 copy.187
  254.5 1.4 fusion.52
  255.9 2.8 fusion.58
  258.8 0.4 fusion.11
  259.8 2.3 fusion.6
  262.1 0.9 pad_maximum_fusion.2
  263.0 11.2 %all-to-all-start.2 = ((f32[16,65,128]{2,1,0:T(8,128)}), f32[16,65,128]{2,1,0:T(8,128)S(1)}, u32[]{:S(2)}, u32[]{:S(2)}) async-start(f32[16,65,128]{2,1,0:T(8,128)} %pad_maximum_fusion.2), calls=%async_computation.2 | async-start | bytes 1179648 | tf_op jit(solution)/shard_map/all_to_all | solution.py:487
  274.4 0.7 copy.172
  275.1 14.7 %all-to-all-done.2 = f32[16,65,128]{2,1,0:T(8,128)S(1)} async-done(((f32[16,65,128]{2,1,0:T(8,128)}), f32[16,65,128]{2,1,0:T(8,128)S(1)}, u32[]{:S(2)}, u32[]{:S(2)}) %all-to-all-start.2) | async-done | bytes 532512 | tf_op jit(solution)/shard_map/all_to_all | solution.py:487
  290.3 0.7 fusion.35
  291.0 1.3 copy.208
  (87 shorter events, 4.9 us)
Async XLA Ops:
  191.8 1.0 copy-start.4
  198.3 9.9 %all-to-all-start.1 = ((bf16[16,2,32]{2,1,0:T(2,128)(2,1)}), bf16[16,2,32]{2,1,0:T(2,128)(2,1)S(1)}, u32[]{:S(2)}, u32[]{:S(2)}) async-start(bf16[16,2,32]{2,1,0:T(2,128)(2,1)} %bitcast.10), calls=%async_computation.1 | async-start | bytes 16384 | tf_op jit(solution)/shard_map/all_to_all | solution.py:426
  208.2 4.6 %copy-start.10 = (bf16[32,16]{0,1:T(8,128)(2,1)S(1)}, bf16[32,16]{0,1:T(8,128)(2,1)}, u32[]{:S(2)}) copy-start(bf16[32,16]{0,1:T(8,128)(2,1)} %param.28) | copy-start | bytes 3076
  208.2 45.7 %all-to-all-start = ((bf16[16,2,16,2048]{3,2,1,0:T(8,128)(2,1)}), bf16[16,2,16,2048]{3,2,1,0:T(8,128)(2,1)S(1)}, u32[]{:S(2)}, u32[]{:S(2)}) async-start(bf16[16,2,16,2048]{3,2,1,0:T(8,128)(2,1)} %bitcast.148), calls=%async_computation | async-start | bytes 4194304 | tf_op jit(solution)/shard_map/all_to_all | solution.py:425
  214.2 3.9 %copy-start.11 = (s32[32,1]{0,1:T(1,128)S(1)}, s32[32,1]{0,1:T(1,128)}, u32[]{:S(2)}) copy-start(s32[32,1]{0,1:T(1,128)} %param.29) | copy-start | bytes 388
  217.9 1.6 copy-start
  219.5 1.4 copy-start.7
  226.3 3.8 %copy-start.1 = (f32[16,8,8]{0,2,1:T(8,128)}, f32[16,8,8]{0,2,1:T(8,128)S(1)}, u32[]{:S(2)}) copy-start(f32[16,8,8]{0,2,1:T(8,128)S(1)} %select_reduce_fusion) | copy-start | bytes 12292
  228.1 2.0 copy-start.3
  258.7 0.8 copy-start.2
  258.7 0.8 copy-start.6
  258.7 1.1 copy-start.8
  262.1 12.1 %copy-start.9 = (bf16[1,2048]{1,0:T(2,128)(2,1)S(1)}, bf16[1,2048]{1,0:T(2,128)(2,1)}, u32[]{:S(2)}) copy-start(bf16[1,2048]{1,0:T(2,128)(2,1)} %param.22) | copy-start | bytes 12292
  262.1 12.1 %copy-start.5 = (f32[1,8192]{1,0:T(1,128)S(1)}, f32[1,8192]{1,0:T(1,128)}, u32[]{:S(2)}) copy-start(f32[1,8192]{1,0:T(1,128)} %get-tuple-element.40) | copy-start | bytes 98308
  263.0 26.8 %all-to-all-start.2 = ((f32[16,65,128]{2,1,0:T(8,128)}), f32[16,65,128]{2,1,0:T(8,128)S(1)}, u32[]{:S(2)}, u32[]{:S(2)}) async-start(f32[16,65,128]{2,1,0:T(8,128)} %pad_maximum_fusion.2), calls=%async_computation.2 | async-start | bytes 1179648 | tf_op jit(solution)/shard_map/all_to_all | solution.py:487

commit v2 on v1

--- a/solution.py
+++ b/solution.py
@@ -121,29 +121,38 @@
     own_img = pltpu.make_async_copy(payload, ibuf.at[r], loc.at[1])
     own_img.start()
 
-    def piece(zz, core):
-        return wq.at[pl.ds(pl.multiple_of((zz * 2 + core) * half, half), half), :]
-
-    own_rows = w_kv.at[pl.ds(pl.multiple_of(x * half, half), half), :]
-    own_w = pltpu.make_async_copy(own_rows, piece(z, c), loc.at[2])
-    own_w.start()
-
-    def z_copy(way, t, src, zz):
+    kv_width = w_kv.shape[1]
+    side = kv_width // 2
+
+    def piece(h, zz, core):
+        at = pl.multiple_of((zz * 2 + core) * half, half)
+        return wq.at[pl.ds(at, half), h * side : (h + 1) * side]
+
+    def own_rows(h):
+        return w_kv.at[pl.ds(pl.multiple_of(x * half, half), half), h * side : (h + 1) * side]
+
+    own_w = [pltpu.make_async_copy(own_rows(h), piece(h, z, c), loc.at[2 + h]) for h in range(2)]
+
+    def z_copy(h, way, t, src, zz):
         role = ((z + (1 if way == 0 else nz - 1)) % nz) * 4 + y * 2 + c
-        return rdma(src, piece(zz, c), z_s.at[way, t], z_r.at[way, t], x, role)
-
-    def w_sib(i, src, zz):
-        return rdma(src, piece(zz, c), ws_s.at[i], ws_r.at[i], x, sib)
-
-    @pl.when(z < nz - 1)
-    def _():
-        z_copy(0, 1, own_rows, z).start()
-
-    @pl.when(z > 0)
-    def _():
-        z_copy(1, 1, own_rows, z).start()
-
-    w_sib(0, own_rows, z).start()
+        return rdma(src, piece(h, zz, c), z_s.at[h, way, t], z_r.at[h, way, t], x, role)
+
+    def w_sib(h, i, src, zz):
+        return rdma(src, piece(h, zz, c), ws_s.at[h, i], ws_r.at[h, i], x, sib)
+
+    def launch(h):
+        @pl.when(z < nz - 1)
+        def _():
+            z_copy(h, 0, 1, own_rows(h), z).start()
+
+        @pl.when(z > 0)
+        def _():
+            z_copy(h, 1, 1, own_rows(h), z).start()
+
+        own_w[h].start()
+        w_sib(h, 0, own_rows(h), z).start()
+
+    launch(0)
 
     def norm_rows(i, carry):
         at = pl.multiple_of(i * 16, 16)
@@ -219,28 +228,30 @@
     own_m.start()
     own_m.wait()
 
-    def hop(t):
+    def hop(h, t):
         @pl.when(z - t >= 0)
         def _():
-            z_copy(0, t, own_rows, z - t).wait_recv()
+            z_copy(h, 0, t, own_rows(h), z - t).wait_recv()
 
             @pl.when(z < nz - 1)
             def _():
-                z_copy(0, t + 1, piece(z - t, c), z - t).start()
-
-            w_sib(t, piece(z - t, c), z - t).start()
+                z_copy(h, 0, t + 1, piece(h, z - t, c), z - t).start()
+
+            w_sib(h, t, piece(h, z - t, c), z - t).start()
 
         @pl.when(z + t < nz)
         def _():
-            z_copy(1, t, own_rows, z + t).wait_recv()
+            z_copy(h, 1, t, own_rows(h), z + t).wait_recv()
 
             @pl.when(z > 0)
             def _():
-                z_copy(1, t + 1, piece(z + t, c), z + t).start()
-
-            w_sib(nz - 1 + t, piece(z + t, c), z + t).start()
-
-    hop(1)
+                z_copy(h, 1, t + 1, piece(h, z + t, c), z + t).start()
+
+            w_sib(h, nz - 1 + t, piece(h, z + t, c), z + t).start()
+
+    hop(0, 1)
+    if nz == 2:
+        launch(1)
     for k in range(1, n):
         src = (r + n - k) % n
         rdma(mout.at[src], mbuf.at[src], mrg_s.at[k], mrg_r.at[k], x, sib).wait_recv()
@@ -258,22 +269,21 @@
         a_copy(d, 0, rows_i, ai_s, ai_r).start()
 
     for t in range(2, nz):
-        hop(t)
-    own_w.wait()
-    w_sib(0, own_rows, z).wait_recv()
-    for t in range(1, nz):
-        @pl.when(z - t >= 0)
-        def _():
-            w_sib(t, own_rows, z - t).wait_recv()
-
-        @pl.when(z + t < nz)
-        def _():
-            w_sib(nz - 1 + t, own_rows, z + t).wait_recv()
-
-    kv_width = w_kv.shape[1]
-    for d in range(1, 4):
-        a_copy(d, rows_i, rows_t, at_s, at_r).wait()
-        a_copy(d, 0, rows_i, ai_s, ai_r).wait()
+        hop(0, t)
+        if t == max(nz - 2, 2):
+            launch(1)
+
+    def settled(h):
+        own_w[h].wait()
+        w_sib(h, 0, own_rows(h), z).wait_recv()
+        for t in range(1, nz):
+            @pl.when(z - t >= 0)
+            def _():
+                w_sib(h, t, own_rows(h), z - t).wait_recv()
+
+            @pl.when(z + t < nz)
+            def _():
+                w_sib(h, nz - 1 + t, own_rows(h), z + t).wait_recv()
 
     def c_copy(d, j):
         _, ox, role = member(d)
@@ -281,26 +291,19 @@
 
     parts = kv_width // CHUNK
 
-    def partials(j, carry):
-        cols = pl.ds(pl.multiple_of(j * CHUNK, CHUNK), CHUNK)
+    def partials(j):
         for d in (3, 1, 2):
             csend[d - 1, j] = jnp.dot(
-                arecv[d - 1], wq[:, cols], preferred_element_type=jnp.float32
+                arecv[d - 1], wq[:, j * CHUNK : (j + 1) * CHUNK], preferred_element_type=jnp.float32
             ).astype(jnp.bfloat16)
             c_copy(d, j).start()
-        return carry
-
-    lax.fori_loop(0, parts, partials, 0)
-
-    def own_partial(j, carry):
-        cols = pl.ds(pl.multiple_of(j * CHUNK, CHUNK), CHUNK)
+
+    def own_partial(j):
+        cols = slice(j * CHUNK, (j + 1) * CHUNK)
         projected[:, cols] = jnp.dot(abuf[mine], wq[:, cols], preferred_element_type=jnp.float32)
-        return carry
-
-    lax.fori_loop(0, parts, own_partial, 0)
-
-    def add_partials(j, carry):
-        cols = pl.ds(pl.multiple_of(j * CHUNK, CHUNK), CHUNK)
+
+    def add_partials(j):
+        cols = slice(j * CHUNK, (j + 1) * CHUNK)
         for d in range(1, 4):
             c_copy(d, j).wait()
         projected[:, cols] = (
@@ -309,9 +312,31 @@
             + crecv[1, j].astype(jnp.float32)
             + crecv[2, j].astype(jnp.float32)
         )
-        return carry
-
-    lax.fori_loop(0, parts, add_partials, 0)
+
+    for d in range(1, 4):
+        a_copy(d, rows_i, rows_t, at_s, at_r).wait()
+        a_copy(d, 0, rows_i, ai_s, ai_r).wait()
+    settled(0)
+    early = range(parts // 2)
+    late = range(parts // 2, parts)
+    hops = list(range(1, nz))
+    for j in early:
+        partials(j)
+        if hops:
+            hop(1, hops.pop(0))
+    if hops:
+        hop(1, hops.pop(0))
+    for j in early:
+        own_partial(j)
+    for t in hops:
+        hop(1, t)
+    settled(1)
+    for j in late:
+        partials(j)
+    for j in late:
+        own_partial(j)
+    for j in range(parts):
+        add_partials(j)
 
     for k in range(1, chips):
         img_copy(k).wait_send()
@@ -319,23 +344,24 @@
         rdma(payload, ibuf.at[r], sib_s.at[k], sib_r.at[k], x, sib).wait_send()
     for k in range(1, n):
         rdma(mout.at[r], mbuf.at[r], mrg_s.at[k], mrg_r.at[k], x, sib).wait_send()
-    w_sib(0, own_rows, z).wait_send()
-    for t in range(1, nz):
-        @pl.when((z - t + 1 >= 0) & (z < nz - 1))
-        def _():
-            z_copy(0, t, own_rows, z).wait_send()
-
-        @pl.when((z + t - 1 < nz) & (z > 0))
-        def _():
-            z_copy(1, t, own_rows, z).wait_send()
-
-        @pl.when(z - t >= 0)
-        def _():
-            w_sib(t, own_rows, z).wait_send()
-
-        @pl.when(z + t < nz)
-        def _():
-            w_sib(nz - 1 + t, own_rows, z).wait_send()
+    for h in range(2):
+        w_sib(h, 0, own_rows(h), z).wait_send()
+        for t in range(1, nz):
+            @pl.when((z - t + 1 >= 0) & (z < nz - 1))
+            def _():
+                z_copy(h, 0, t, own_rows(h), z).wait_send()
+
+            @pl.when((z + t - 1 < nz) & (z > 0))
+            def _():
+                z_copy(h, 1, t, own_rows(h), z).wait_send()
+
+            @pl.when(z - t >= 0)
+            def _():
+                w_sib(h, t, own_rows(h), z).wait_send()
+
+            @pl.when(z + t < nz)
+            def _():
+                w_sib(h, nz - 1 + t, own_rows(h), z).wait_send()
 
 
 def front(payload, vis_gain, w_merge, text, norm_gain, w_kv):
@@ -374,8 +400,8 @@
             pltpu.VMEM((3, parts, length, CHUNK), bf),
             dma((chips,)), dma((chips,)), dma((chips,)), dma((chips,)),
             dma((n,)), dma((n,)), dma((3,)), dma((3,)), dma((3,)), dma((3,)),
-            dma((2, nz + 1)), dma((2, nz + 1)), dma((2 * nz,)), dma((2 * nz,)),
-            dma((3, parts)), dma((3, parts)), dma((3,)),
+            dma((2, 2, nz + 1)), dma((2, 2, nz + 1)), dma((2, 2 * nz)), dma((2, 2 * nz)),
+            dma((3, parts)), dma((3, parts)), dma((4,)),
         ],
         compiler_params=pltpu.CompilerParams(
             collective_id=0, has_side_effects=True, vmem_limit_bytes=56 * 1024 * 1024

time: 293 us -> 269 us (0.918)
  Pallas kernels: 181 us -> 157 us
    pallas_call x1, Pallas kernels: 181 us -> 157 us  [front(): pl.pallas_call(functools.partial(front_kernel, n), out_shape=(jax.ShapeDt...]
where the time goes in v2:
time: 269 us; the launch traced here: 268 us
  Pallas kernels  157 us (58%)
  waiting for transfers between devices  36.5 us (14%)
  local copies, waits for them, and re-layouts  25.8 us (10%)
  starting transfers between devices  19.3 us (7%)
  other arithmetic  16.1 us (6%)
  matrix products  12.1 us (4%)
    pallas_call x1, Pallas kernels, front(): pl.pallas_call(functools.partial(front_kernel, n), out_shape=(jax.ShapeDt...  157 us
    all_to_all x1, waiting for transfers between devices, tail(): lax.all_to_all(send_quant, 'role', split_axis=0, concat_axis=0, tiled=True)  20.3 us
    unnamed x39, local copies, waits for them, and re-layouts  18 us
    all_to_all x1, waiting for transfers between devices, tail(): lax.all_to_all(packed, 'role', split_axis=0, concat_axis=0, tiled=True)  14.7 us
    all_to_all x1, starting transfers between devices, tail(): lax.all_to_all(packed, 'role', split_axis=0, concat_axis=0, tiled=True)  11.2 us
  transfers between devices with their start and end apart: 3, of which 3 were waited for; matrix products, arithmetic and copies ran while one was open for 9% of the time, Pallas kernels for 0%

profile of v2, /device:TPU:0, one launch (start us, length us, event | category | flops | bytes accessed | tf_op | source)
XLA Modules:
  0.0 268.5 jit_solution(17410682290448769878)
XLA Ops:
  1.3 0.7 convert.17
  2.0 0.7 convert_bitcast_fusion
  2.7 0.7 fusion.37
  3.4 0.8 select_reduce_fusion.2
  4.3 0.7 multiply_add_fusion.2
  4.9 1.5 fusion.54
  6.6 1.6 pad_maximum_fusion.3.payload
  8.2 157.0 %front.1 = (f32[272,2048]{1,0:T(8,128)}, bf16[16,16,640]{2,1,0:T(8,128)(2,1)}) custom-call(bf16[16,5760]{1,0:T(8,128)(2,1)} %pad_maximum_fusion.3.payload, f32[1,5120]{1,0:T(1,128)} %bitcast.172, bf16[5120,512]{1,0:T(8,128)(2,1)} %w_merge.1, bf16[240,8192]{1,0:T(8,128)(2,1)} %text.1, f32[1,8192]{1,0:T(1,128)} %bitcast.170, bf16[512,2048]{1,0:T(8,128)(2,1)} %w_kv.1), custom_call_target="tpu_custom_call" | custom-call | tf_op jit(solution)/shard_map/front/pallas_call | solution.py:382
  165.2 2.8 %slice_bitcast_fusion.1 = (f32[34,8,8,128]{3,1,2,0:T(8,128)S(1)}, f32[34,8,8,128]{3,1,2,0:T(8,128)}) fusion(f32[272,2048]{1,0:T(8,128)} %get-tuple-element.5), kind=kLoop, calls=%fused_computation.19 | loop fusion | bytes 4456448
  168.2 0.8 copy-done.4
  170.5 1.5 copy.184
  172.0 0.6 multiply_cosine_fusion
  172.5 0.6 multiply_subtract_fusion
  173.1 0.4 pad_maximum_fusion.1
  173.8 0.7 convolution_convert_fusion.2
  174.5 3.5 %all-to-all-start.1 = ((bf16[16,2,32]{2,1,0:T(2,128)(2,1)}), bf16[16,2,32]{2,1,0:T(2,128)(2,1)S(1)}, u32[]{:S(2)}, u32[]{:S(2)}) async-start(bf16[16,2,32]{2,1,0:T(2,128)(2,1)} %bitcast.10), calls=%async_computation.1 | async-start | bytes 16384 | tf_op jit(solution)/shard_map/all_to_all | solution.py:452
  178.6 1.0 copy.185
  179.6 0.7 convolution_convert_fusion
  180.3 2.5 copy.186
  182.8 1.6 all-to-all-done.1
  184.4 4.6 %all-to-all-start = ((bf16[16,2,16,2048]{3,2,1,0:T(8,128)(2,1)}), bf16[16,2,16,2048]{3,2,1,0:T(8,128)(2,1)S(1)}, u32[]{:S(2)}, u32[]{:S(2)}) async-start(bf16[16,2,16,2048]{3,2,1,0:T(8,128)(2,1)} %bitcast.148), calls=%async_computation | async-start | bytes 4194304 | tf_op jit(solution)/shard_map/all_to_all | solution.py:451
  189.0 0.7 copy.180
  189.7 0.7 copy.179
  190.4 3.6 %copy.190 = bf16[64,8,16,128]{3,2,1,0:T(8,128)(2,1)} copy(bf16[64,8,16,128]{3,1,2,0:T(8,128)(2,1)} %bitcast.156) | data formatting | bytes 4194304
  194.3 0.3 fusion.3
  194.8 1.0 copy-done
  195.7 1.4 fusion.51
  197.1 0.8 fusion.57
  197.8 0.7 copy.158
  198.6 1.3 fusion.10
  199.9 1.6 copy.169
  201.5 1.0 select_reduce_fusion
  202.5 1.8 fusion.16
  204.3 2.0 fusion.7
  206.3 2.4 fusion.8
  208.8 0.7 copy.154
  209.8 20.3 %all-to-all-done = bf16[16,2,16,2048]{3,2,1,0:T(8,128)(2,1)S(1)} async-done(((bf16[16,2,16,2048]{3,2,1,0:T(8,128)(2,1)}), bf16[16,2,16,2048]{3,2,1,0:T(8,128)(2,1)S(1)}, u32[]{:S(2)}, u32[]{:S(2)}) %all-to-all-start) | async-done | bytes 2097184 | tf_op jit(solution)/shard_map/all_to_all | solution.py:451
  230.1 0.6 copy.187
  230.7 1.4 fusion.52
  232.0 2.8 %fusion.58 = (f32[16,8,8]{2,1,0:T(8,128)S(1)}, f32[16,8,8,2,16]{4,2,3,1,0:T(8,128)S(1)}) fusion(f32[16,8,2]{2,1,0:T(8,128)S(1)} %copy.153, bf16[16,2,16,1,8,128]{5,4,3,2,1,0:T(8,128)(2,1)S(1)} %get-tuple-element.31, bf16[16,8,8,128,1]{3,2,1,0,4:T(8,128)(2,1)S(1)} %reshape.434, pred[16,2,16]{2,1,0:T(4,128)(4,1)S(1)} %convert_compare_fusion), kind=kOutput, calls=%fused_computation.128 | convolution fusion | flops 8518656 | bytes 1447424 | tf_op jit(solution)/shard_map/scbkd,skgd->skgcb/dot_general | solution.py:488
  235.0 0.4 fusion.11
  236.0 2.3 fusion.6
  238.3 0.9 pad_maximum_fusion.2
  239.2 11.2 %all-to-all-start.2 = ((f32[16,65,128]{2,1,0:T(8,128)}), f32[16,65,128]{2,1,0:T(8,128)S(1)}, u32[]{:S(2)}, u32[]{:S(2)}) async-start(f32[16,65,128]{2,1,0:T(8,128)} %pad_maximum_fusion.2), calls=%async_computation.2 | async-start | bytes 1179648 | tf_op jit(solution)/shard_map/all_to_all | solution.py:513
  250.6 0.7 copy.172
  251.3 14.7 %all-to-all-done.2 = f32[16,65,128]{2,1,0:T(8,128)S(1)} async-done(((f32[16,65,128]{2,1,0:T(8,128)}), f32[16,65,128]{2,1,0:T(8,128)S(1)}, u32[]{:S(2)}, u32[]{:S(2)}) %all-to-all-start.2) | async-done | bytes 532512 | tf_op jit(solution)/shard_map/all_to_all | solution.py:513
  266.5 0.7 fusion.35
  267.1 1.3 copy.208
  (87 shorter events, 4.9 us)
Async XLA Ops:
  168.0 1.0 copy-start.4
  174.5 9.9 %all-to-all-start.1 = ((bf16[16,2,32]{2,1,0:T(2,128)(2,1)}), bf16[16,2,32]{2,1,0:T(2,128)(2,1)S(1)}, u32[]{:S(2)}, u32[]{:S(2)}) async-start(bf16[16,2,32]{2,1,0:T(2,128)(2,1)} %bitcast.10), calls=%async_computation.1 | async-start | bytes 16384 | tf_op jit(solution)/shard_map/all_to_all | solution.py:452
  184.4 4.6 %copy-start.10 = (bf16[32,16]{0,1:T(8,128)(2,1)S(1)}, bf16[32,16]{0,1:T(8,128)(2,1)}, u32[]{:S(2)}) copy-start(bf16[32,16]{0,1:T(8,128)(2,1)} %param.28) | copy-start | bytes 3076
  184.4 45.7 %all-to-all-start = ((bf16[16,2,16,2048]{3,2,1,0:T(8,128)(2,1)}), bf16[16,2,16,2048]{3,2,1,0:T(8,128)(2,1)S(1)}, u32[]{:S(2)}, u32[]{:S(2)}) async-start(bf16[16,2,16,2048]{3,2,1,0:T(8,128)(2,1)} %bitcast.148), calls=%async_computation | async-start | bytes 4194304 | tf_op jit(solution)/shard_map/all_to_all | solution.py:451
  190.4 3.9 %copy-start.11 = (s32[32,1]{0,1:T(1,128)S(1)}, s32[32,1]{0,1:T(1,128)}, u32[]{:S(2)}) copy-start(s32[32,1]{0,1:T(1,128)} %param.29) | copy-start | bytes 388
  194.1 1.6 copy-start
  195.7 1.4 copy-start.7
  202.5 3.8 %copy-start.1 = (f32[16,8,8]{0,2,1:T(8,128)}, f32[16,8,8]{0,2,1:T(8,128)S(1)}, u32[]{:S(2)}) copy-start(f32[16,8,8]{0,2,1:T(8,128)S(1)} %select_reduce_fusion) | copy-start | bytes 12292
  204.3 2.0 copy-start.3
  234.9 0.8 copy-start.2
  234.9 0.8 copy-start.6
  234.9 1.1 copy-start.8
  238.3 12.1 %copy-start.9 = (bf16[1,2048]{1,0:T(2,128)(2,1)S(1)}, bf16[1,2048]{1,0:T(2,128)(2,1)}, u32[]{:S(2)}) copy-start(bf16[1,2048]{1,0:T(2,128)(2,1)} %param.22) | copy-start | bytes 12292
  238.3 12.1 %copy-start.5 = (f32[1,8192]{1,0:T(1,128)S(1)}, f32[1,8192]{1,0:T(1,128)}, u32[]{:S(2)}) copy-start(f32[1,8192]{1,0:T(1,128)} %get-tuple-element.40) | copy-start | bytes 98308
  239.2 26.8 %all-to-all-start.2 = ((f32[16,65,128]{2,1,0:T(8,128)}), f32[16,65,128]{2,1,0:T(8,128)S(1)}, u32[]{:S(2)}, u32[]{:S(2)}) async-start(f32[16,65,128]{2,1,0:T(8,128)} %pad_maximum_fusion.2), calls=%async_computation.2 | async-start | bytes 1179648 | tf_op jit(solution)/shard_map/all_to_all | solution.py:513

commit v3 on v2

--- a/solution.py
+++ b/solution.py
@@ -122,7 +122,8 @@
     own_img.start()
 
     kv_width = w_kv.shape[1]
-    side = kv_width // 2
+    side = CHUNK
+    parts = kv_width // CHUNK
 
     def piece(h, zz, core):
         at = pl.multiple_of((zz * 2 + core) * half, half)
@@ -131,7 +132,7 @@
     def own_rows(h):
         return w_kv.at[pl.ds(pl.multiple_of(x * half, half), half), h * side : (h + 1) * side]
 
-    own_w = [pltpu.make_async_copy(own_rows(h), piece(h, z, c), loc.at[2 + h]) for h in range(2)]
+    own_w = [pltpu.make_async_copy(own_rows(h), piece(h, z, c), loc.at[2 + h]) for h in range(parts)]
 
     def z_copy(h, way, t, src, zz):
         role = ((z + (1 if way == 0 else nz - 1)) % nz) * 4 + y * 2 + c
@@ -250,8 +251,7 @@
             w_sib(h, nz - 1 + t, piece(h, z + t, c), z + t).start()
 
     hop(0, 1)
-    if nz == 2:
-        launch(1)
+    launch(1)
     for k in range(1, n):
         src = (r + n - k) % n
         rdma(mout.at[src], mbuf.at[src], mrg_s.at[k], mrg_r.at[k], x, sib).wait_recv()
@@ -270,8 +270,6 @@
 
     for t in range(2, nz):
         hop(0, t)
-        if t == max(nz - 2, 2):
-            launch(1)
 
     def settled(h):
         own_w[h].wait()
@@ -316,25 +314,16 @@
     for d in range(1, 4):
         a_copy(d, rows_i, rows_t, at_s, at_r).wait()
         a_copy(d, 0, rows_i, ai_s, ai_r).wait()
-    settled(0)
-    early = range(parts // 2)
-    late = range(parts // 2, parts)
-    hops = list(range(1, nz))
-    for j in early:
-        partials(j)
-        if hops:
-            hop(1, hops.pop(0))
-    if hops:
-        hop(1, hops.pop(0))
-    for j in early:
-        own_partial(j)
-    for t in hops:
-        hop(1, t)
-    settled(1)
-    for j in late:
-        partials(j)
-    for j in late:
-        own_partial(j)
+    for h in range(parts):
+        settled(h)
+        partials(h)
+        for t in range(1, nz):
+            if t == nz - 1:
+                own_partial(h)
+            if h + 1 < parts:
+                hop(h + 1, t)
+                if t == 1 and h + 2 < parts:
+                    launch(h + 2)
     for j in range(parts):
         add_partials(j)
 
@@ -344,7 +333,7 @@
         rdma(payload, ibuf.at[r], sib_s.at[k], sib_r.at[k], x, sib).wait_send()
     for k in range(1, n):
         rdma(mout.at[r], mbuf.at[r], mrg_s.at[k], mrg_r.at[k], x, sib).wait_send()
-    for h in range(2):
+    for h in range(parts):
         w_sib(h, 0, own_rows(h), z).wait_send()
         for t in range(1, nz):
             @pl.when((z - t + 1 >= 0) & (z < nz - 1))
@@ -400,8 +389,8 @@
             pltpu.VMEM((3, parts, length, CHUNK), bf),
             dma((chips,)), dma((chips,)), dma((chips,)), dma((chips,)),
             dma((n,)), dma((n,)), dma((3,)), dma((3,)), dma((3,)), dma((3,)),
-            dma((2, 2, nz + 1)), dma((2, 2, nz + 1)), dma((2, 2 * nz)), dma((2, 2 * nz)),
-            dma((3, parts)), dma((3, parts)), dma((4,)),
+            dma((parts, 2, nz + 1)), dma((parts, 2, nz + 1)), dma((parts, 2 * nz)), dma((parts, 2 * nz)),
+            dma((3, parts)), dma((3, parts)), dma((2 + parts,)),
         ],
         compiler_params=pltpu.CompilerParams(
             collective_id=0, has_side_effects=True, vmem_limit_bytes=56 * 1024 * 1024

time: 269 us -> 264 us (0.981)
  Pallas kernels: 157 us -> 152 us
    pallas_call x1, Pallas kernels: 157 us -> 152 us  [front(): pl.pallas_call(functools.partial(front_kernel, n), out_shape=(jax.ShapeDt...]
  transfers between devices with their start and end apart: 3 -> 3, of which waited for: 3 -> 3; matrix products, arithmetic and copies ran while one was open for 9% -> 10% of each run, Pallas kernels for 0% -> 0%
where the time goes in v3:
time: 264 us; the launch traced here: 263 us
  Pallas kernels  152 us (58%)
  waiting for transfers between devices  36.5 us (14%)
  local copies, waits for them, and re-layouts  25.8 us (10%)
  starting transfers between devices  19.3 us (7%)
  other arithmetic  16.1 us (6%)
  matrix products  12.1 us (5%)
    pallas_call x1, Pallas kernels, front(): pl.pallas_call(functools.partial(front_kernel, n), out_shape=(jax.ShapeDt...  152 us
    all_to_all x1, waiting for transfers between devices, tail(): lax.all_to_all(send_quant, 'role', split_axis=0, concat_axis=0, tiled=True)  20.3 us
    unnamed x39, local copies, waits for them, and re-layouts  18 us
    all_to_all x1, waiting for transfers between devices, tail(): lax.all_to_all(packed, 'role', split_axis=0, concat_axis=0, tiled=True)  14.7 us
    all_to_all x1, starting transfers between devices, tail(): lax.all_to_all(packed, 'role', split_axis=0, concat_axis=0, tiled=True)  11.2 us
  transfers between devices with their start and end apart: 3, of which 3 were waited for; matrix products, arithmetic and copies ran while one was open for 10% of the time, Pallas kernels for 0%

profile of v3, /device:TPU:0, one launch (start us, length us, event | category | flops | bytes accessed | tf_op | source)
XLA Modules:
  0.0 263.1 jit_solution(16391289439156834240)
XLA Ops:
  1.3 0.7 convert.17
  2.0 0.7 convert_bitcast_fusion
  2.7 0.7 fusion.37
  3.4 0.8 select_reduce_fusion.2
  4.3 0.7 multiply_add_fusion.2
  4.9 1.5 fusion.54
  6.6 1.6 pad_maximum_fusion.3.payload
  8.2 151.6 %front.1 = (f32[272,2048]{1,0:T(8,128)}, bf16[16,16,640]{2,1,0:T(8,128)(2,1)}) custom-call(bf16[16,5760]{1,0:T(8,128)(2,1)} %pad_maximum_fusion.3.payload, f32[1,5120]{1,0:T(1,128)} %bitcast.172, bf16[5120,512]{1,0:T(8,128)(2,1)} %w_merge.1, bf16[240,8192]{1,0:T(8,128)(2,1)} %text.1, f32[1,8192]{1,0:T(1,128)} %bitcast.170, bf16[512,2048]{1,0:T(8,128)(2,1)} %w_kv.1), custom_call_target="tpu_custom_call" | custom-call | tf_op jit(solution)/shard_map/front/pallas_call | solution.py:371
  159.9 2.8 %slice_bitcast_fusion.1 = (f32[34,8,8,128]{3,1,2,0:T(8,128)S(1)}, f32[34,8,8,128]{3,1,2,0:T(8,128)}) fusion(f32[272,2048]{1,0:T(8,128)} %get-tuple-element.5), kind=kLoop, calls=%fused_computation.19 | loop fusion | bytes 4456448
  162.9 0.8 copy-done.4
  165.1 1.5 copy.184
  166.6 0.6 multiply_cosine_fusion
  167.1 0.6 multiply_subtract_fusion
  167.7 0.4 pad_maximum_fusion.1
  168.4 0.7 convolution_convert_fusion.2
  169.1 3.5 %all-to-all-start.1 = ((bf16[16,2,32]{2,1,0:T(2,128)(2,1)}), bf16[16,2,32]{2,1,0:T(2,128)(2,1)S(1)}, u32[]{:S(2)}, u32[]{:S(2)}) async-start(bf16[16,2,32]{2,1,0:T(2,128)(2,1)} %bitcast.10), calls=%async_computation.1 | async-start | bytes 16384 | tf_op jit(solution)/shard_map/all_to_all | solution.py:441
  173.2 1.0 copy.185
  174.2 0.7 convolution_convert_fusion
  175.0 2.5 copy.186
  177.5 1.6 all-to-all-done.1
  179.0 4.6 %all-to-all-start = ((bf16[16,2,16,2048]{3,2,1,0:T(8,128)(2,1)}), bf16[16,2,16,2048]{3,2,1,0:T(8,128)(2,1)S(1)}, u32[]{:S(2)}, u32[]{:S(2)}) async-start(bf16[16,2,16,2048]{3,2,1,0:T(8,128)(2,1)} %bitcast.148), calls=%async_computation | async-start | bytes 4194304 | tf_op jit(solution)/shard_map/all_to_all | solution.py:440
  183.6 0.7 copy.180
  184.3 0.7 copy.179
  185.0 3.6 %copy.190 = bf16[64,8,16,128]{3,2,1,0:T(8,128)(2,1)} copy(bf16[64,8,16,128]{3,1,2,0:T(8,128)(2,1)} %bitcast.156) | data formatting | bytes 4194304
  188.9 0.3 fusion.3
  189.4 1.0 copy-done
  190.3 1.4 fusion.51
  191.7 0.8 fusion.57
  192.5 0.7 copy.158
  193.2 1.3 fusion.10
  194.5 1.6 copy.169
  196.1 1.0 select_reduce_fusion
  197.1 1.8 fusion.16
  198.9 2.0 fusion.7
  200.9 2.4 fusion.8
  203.4 0.7 copy.154
  204.4 20.3 %all-to-all-done = bf16[16,2,16,2048]{3,2,1,0:T(8,128)(2,1)S(1)} async-done(((bf16[16,2,16,2048]{3,2,1,0:T(8,128)(2,1)}), bf16[16,2,16,2048]{3,2,1,0:T(8,128)(2,1)S(1)}, u32[]{:S(2)}, u32[]{:S(2)}) %all-to-all-start) | async-done | bytes 2097184 | tf_op jit(solution)/shard_map/all_to_all | solution.py:440
  224.7 0.6 copy.187
  225.3 1.4 fusion.52
  226.7 2.8 %fusion.58 = (f32[16,8,8]{2,1,0:T(8,128)S(1)}, f32[16,8,8,2,16]{4,2,3,1,0:T(8,128)S(1)}) fusion(f32[16,8,2]{2,1,0:T(8,128)S(1)} %copy.153, bf16[16,2,16,1,8,128]{5,4,3,2,1,0:T(8,128)(2,1)S(1)} %get-tuple-element.31, bf16[16,8,8,128,1]{3,2,1,0,4:T(8,128)(2,1)S(1)} %reshape.434, pred[16,2,16]{2,1,0:T(4,128)(4,1)S(1)} %convert_compare_fusion), kind=kOutput, calls=%fused_computation.128 | convolution fusion | flops 8518656 | bytes 1447424 | tf_op jit(solution)/shard_map/scbkd,skgd->skgcb/dot_general | solution.py:477
  229.6 0.4 fusion.11
  230.6 2.3 fusion.6
  232.9 0.9 pad_maximum_fusion.2
  233.8 11.2 %all-to-all-start.2 = ((f32[16,65,128]{2,1,0:T(8,128)}), f32[16,65,128]{2,1,0:T(8,128)S(1)}, u32[]{:S(2)}, u32[]{:S(2)}) async-start(f32[16,65,128]{2,1,0:T(8,128)} %pad_maximum_fusion.2), calls=%async_computation.2 | async-start | bytes 1179648 | tf_op jit(solution)/shard_map/all_to_all | solution.py:502
  245.2 0.7 copy.172
  245.9 14.7 %all-to-all-done.2 = f32[16,65,128]{2,1,0:T(8,128)S(1)} async-done(((f32[16,65,128]{2,1,0:T(8,128)}), f32[16,65,128]{2,1,0:T(8,128)S(1)}, u32[]{:S(2)}, u32[]{:S(2)}) %all-to-all-start.2) | async-done | bytes 532512 | tf_op jit(solution)/shard_map/all_to_all | solution.py:502
  261.1 0.7 fusion.35
  261.8 1.3 copy.208
  (87 shorter events, 4.9 us)
Async XLA Ops:
  162.6 1.0 copy-start.4
  169.1 9.9 %all-to-all-start.1 = ((bf16[16,2,32]{2,1,0:T(2,128)(2,1)}), bf16[16,2,32]{2,1,0:T(2,128)(2,1)S(1)}, u32[]{:S(2)}, u32[]{:S(2)}) async-start(bf16[16,2,32]{2,1,0:T(2,128)(2,1)} %bitcast.10), calls=%async_computation.1 | async-start | bytes 16384 | tf_op jit(solution)/shard_map/all_to_all | solution.py:441
  179.0 4.6 %copy-start.10 = (bf16[32,16]{0,1:T(8,128)(2,1)S(1)}, bf16[32,16]{0,1:T(8,128)(2,1)}, u32[]{:S(2)}) copy-start(bf16[32,16]{0,1:T(8,128)(2,1)} %param.28) | copy-start | bytes 3076
  179.0 45.7 %all-to-all-start = ((bf16[16,2,16,2048]{3,2,1,0:T(8,128)(2,1)}), bf16[16,2,16,2048]{3,2,1,0:T(8,128)(2,1)S(1)}, u32[]{:S(2)}, u32[]{:S(2)}) async-start(bf16[16,2,16,2048]{3,2,1,0:T(8,128)(2,1)} %bitcast.148), calls=%async_computation | async-start | bytes 4194304 | tf_op jit(solution)/shard_map/all_to_all | solution.py:440
  185.0 3.9 %copy-start.11 = (s32[32,1]{0,1:T(1,128)S(1)}, s32[32,1]{0,1:T(1,128)}, u32[]{:S(2)}) copy-start(s32[32,1]{0,1:T(1,128)} %param.29) | copy-start | bytes 388
  188.7 1.6 copy-start
  190.3 1.4 copy-start.7
  197.1 3.8 %copy-start.1 = (f32[16,8,8]{0,2,1:T(8,128)}, f32[16,8,8]{0,2,1:T(8,128)S(1)}, u32[]{:S(2)}) copy-start(f32[16,8,8]{0,2,1:T(8,128)S(1)} %select_reduce_fusion) | copy-start | bytes 12292
  198.9 2.0 copy-start.3
  229.5 0.8 copy-start.2
  229.5 0.8 copy-start.6
  229.5 1.1 copy-start.8
  232.9 12.1 %copy-start.9 = (bf16[1,2048]{1,0:T(2,128)(2,1)S(1)}, bf16[1,2048]{1,0:T(2,128)(2,1)}, u32[]{:S(2)}) copy-start(bf16[1,2048]{1,0:T(2,128)(2,1)} %param.22) | copy-start | bytes 12292
  232.9 12.1 %copy-start.5 = (f32[1,8192]{1,0:T(1,128)S(1)}, f32[1,8192]{1,0:T(1,128)}, u32[]{:S(2)}) copy-start(f32[1,8192]{1,0:T(1,128)} %get-tuple-element.40) | copy-start | bytes 98308
  233.8 26.8 %all-to-all-start.2 = ((f32[16,65,128]{2,1,0:T(8,128)}), f32[16,65,128]{2,1,0:T(8,128)S(1)}, u32[]{:S(2)}, u32[]{:S(2)}) async-start(f32[16,65,128]{2,1,0:T(8,128)} %pad_maximum_fusion.2), calls=%async_computation.2 | async-start | bytes 1179648 | tf_op jit(solution)/shard_map/all_to_all | solution.py:502
